TPU v7x, 768 devices: a whole 4x8x12 slice. The times are simulated.
768 devices in a mesh: px: 16 (over y_hi, x, core), py: 48 (over y_lo, z).
Axes of the slice: x: 4, y: 8 (y_hi: 2, y_lo: 4; y = y_hi * 4 + y_lo), z: 12, core: 2. Of those that a mesh axis runs over, the one named last changes fastest.
Arguments:
- features: bfloat16 [64, 384, 128], P('px', 'py'), may hold values from -6 to 6
- pair_mask: int32 [64, 384, 3], P('px', 'py'), may hold values 0 or 1
- w_update: bfloat16 [128, 128], replicated, may hold values from -0.21875 to 0.21875
- w_atom: bfloat16 [128, 128], replicated, may hold values from -0.5 to 0.5
- w_pair: bfloat16 [128, 128], replicated, may hold values from -0.5 to 0.5
- slot_bias: float32 [4, 128], replicated, may hold values from -4 to 4
- w_block: bfloat16 [128, 169], replicated, may hold values from -0.5 to 0.5
- trial: float32 [64, 384, 13, 256], P('px', 'py'), may hold values from -6 to 6
Outputs:
- filtered: float32 [64, 384, 13, 256], P('px', 'py')
All inputs are finite; a program needn't handle non-finite values. No bound on the sum of `pair_mask` on one device may be relied on, other than what follows from the above.
Results may differ from a plain program's by a relative error of at most 0.0046.
Values may be sent and summed in bfloat16 or wider, within the bound.
A program may use at most 64 MiB of HBM per device.

v0:
```python
import jax
import jax.numpy as jnp
from jax import lax
from jax.sharding import PartitionSpec as P

ORBITALS = 13
STEPS = 3


OFFSETS = ((0, 1), (1, 0), (1, 1))
CENTRE = 4.0
HALF_WIDTH = 24.0


def with_halo(cells, sides, width):
    for axis, dim in sides:
        count = lax.axis_size(axis)
        head = lax.slice_in_dim(cells, 0, width, axis=dim)
        tail = lax.slice_in_dim(cells, cells.shape[dim] - width, cells.shape[dim], axis=dim)
        cells = jnp.concatenate(
            [
                lax.ppermute(tail, axis, [(i, (i + 1) % count) for i in range(count)]),
                cells,
                lax.ppermute(head, axis, [((i + 1) % count, i) for i in range(count)]),
            ],
            axis=dim,
        )
    return cells


def shifted(x, axis, by):
    length = lax.axis_size(axis)
    return lax.ppermute(x, axis, [(i, (i + by) % length) for i in range(length)])


def window(values, top, left, height, breadth):
    return values[top : top + height, left : left + breadth]


def contract(blocks, vectors_in):
    return jnp.einsum("xyab,xybv->xyav", blocks, vectors_in, precision=lax.Precision.HIGHEST)


def operate(extended, onsite, forward, backward):
    height = extended.shape[0] - 2
    breadth = extended.shape[1] - 2
    summed = contract(onsite, window(extended, 1, 1, height, breadth))
    for slot in range(3):
        row_step, col_step = OFFSETS[slot]
        summed = summed + contract(
            forward[slot], window(extended, 1 + row_step, 1 + col_step, height, breadth)
        )
        summed = summed + contract(
            jnp.swapaxes(backward[slot], -1, -2),
            window(extended, 1 - row_step, 1 - col_step, height, breadth),
        )
    return summed


def as_matrix(flat):
    return flat.reshape(flat.shape[0], flat.shape[1], ORBITALS, ORBITALS)


def per_device(features, pair_mask, w_update, w_atom, w_pair, slot_bias, w_block, trial):
    height, breadth = (features.shape[0], features.shape[1])
    feature_ext = with_halo(features, (("px", 0), ("py", 1)), 1)
    widened = feature_ext.astype(jnp.float32)
    gathered = jnp.zeros((height, breadth, features.shape[2]), jnp.float32)
    for row_step, col_step in OFFSETS:
        gathered = gathered + window(widened, 1 + row_step, 1 + col_step, height, breadth)
        gathered = gathered + window(widened, 1 - row_step, 1 - col_step, height, breadth)
    update = jax.nn.silu(
        jnp.dot(gathered.astype(jnp.bfloat16), w_update, preferred_element_type=jnp.float32)
    )
    refined = (window(widened, 1, 1, height, breadth) + update).astype(jnp.bfloat16)
    self_part = jnp.dot(refined, w_atom, preferred_element_type=jnp.float32)
    pair_part = jnp.dot(feature_ext, w_pair, preferred_element_type=jnp.float32)
    flat_blocks = []
    for slot in range(3):
        row_step, col_step = OFFSETS[slot]
        message = jax.nn.silu(
            self_part
            + window(pair_part, 1 + row_step, 1 + col_step, height, breadth)
            + slot_bias[slot]
        ).astype(jnp.bfloat16)
        predicted = jnp.dot(message, w_block, preferred_element_type=jnp.float32)
        flat_blocks.append(predicted * pair_mask[:, :, slot : slot + 1].astype(jnp.float32))
    message = jax.nn.silu(
        self_part + window(pair_part, 1, 1, height, breadth) + slot_bias[3]
    ).astype(jnp.bfloat16)
    predicted = as_matrix(jnp.dot(message, w_block, preferred_element_type=jnp.float32))
    onsite_flat = (0.5 * (predicted + jnp.swapaxes(predicted, -1, -2))).reshape(
        height, breadth, ORBITALS * ORBITALS
    )
    forward_stack = jnp.stack(flat_blocks, 2)
    column = shifted(forward_stack[:, -1:], "py", 1)
    widened_blocks = jnp.concatenate([column, forward_stack], 1)
    top_row = shifted(widened_blocks[-1:], "px", 1)
    behind = jnp.concatenate([top_row, widened_blocks], 0)
    forward = [as_matrix(flat_blocks[slot]) for slot in range(3)]
    backward = []
    for slot in range(3):
        row_step, col_step = OFFSETS[slot]
        backward.append(
            as_matrix(window(behind, 1 - row_step, 1 - col_step, height, breadth)[:, :, slot])
        )
    onsite = as_matrix(onsite_flat)

    def scaled(current):
        extended = with_halo(current, (("px", 0), ("py", 1)), 1)
        return (operate(extended, onsite, forward, backward) - CENTRE * current) / HALF_WIDTH

    before = trial
    current = scaled(trial)
    for turn in range(STEPS - 1):
        following = 2.0 * scaled(current) - before
        before, current = (current, following)
    return current


def solution(mesh):
    return jax.shard_map(
        per_device,
        mesh=mesh,
        in_specs=(
            P("px", "py", None),
            P("px", "py", None),
            P(),
            P(),
            P(),
            P(),
            P(),
            P("px", "py", None, None),
        ),
        out_specs=P("px", "py", None, None),
        check_vma=False,
    )
```

profile of v0, /device:TPU:7, one launch (start us, length us, event | category | flops | bytes accessed | tf_op | source)
XLA Modules:
  0.0 148.5 jit_solution(18069587825376866916)
XLA Ops:
  0.0 0.7 fusion.113
  0.7 7.9 %collective-permute-start = (bf16[1,8,128]{2,1,0:T(8,128)(2,1)S(1)}, bf16[1,8,128]{2,1,0:T(8,128)(2,1)S(1)}, u32[]{:S(2)}, u32[]{:S(2)}) collective-permute-start(bf16[1,8,128]{2,1,0:T(8,128)(2,1)S(1)} %get-tuple-element.27), channel_id=1, source_target_pairs={{0,48},{48,96},{96,144},{144,192},{192,240},{240,288},{288,336},{3... | collective-permute-start | bytes 6152 | tf_op jit(solution)/shard_map/ppermute | solution.py:22
  8.6 1.9 %collective-permute-start.1 = (bf16[1,8,128]{2,1,0:T(8,128)(2,1)S(1)}, bf16[1,8,128]{2,1,0:T(8,128)(2,1)S(1)}, u32[]{:S(2)}, u32[]{:S(2)}) collective-permute-start(bf16[1,8,128]{2,1,0:T(8,128)(2,1)S(1)} %get-tuple-element.26), channel_id=1, source_target_pairs={{48,0},{96,48},{144,96},{192,144},{240,192},{288,240},{336,288},{3... | collective-permute-start | bytes 6152 | tf_op jit(solution)/shard_map/ppermute | solution.py:24
  10.6 1.2 copy.29
  11.7 0.7 fusion.111
  12.4 9.6 %collective-permute-start.4 = (f32[1,8,13,256]{3,2,1,0:T(8,128)}, f32[1,8,13,256]{3,2,1,0:T(8,128)S(1)}, u32[]{:S(2)}, u32[]{:S(2)}) collective-permute-start(f32[1,8,13,256]{3,2,1,0:T(8,128)} %get-tuple-element.20), channel_id=1, source_target_pairs={{0,48},{48,96},{96,144},{144,192},{192,240},{240,288},{288,336},{3... | collective-permute-start | bytes 319496 | tf_op jit(solution)/shard_map/ppermute | solution.py:22
  22.1 1.9 %collective-permute-start.5 = (f32[1,8,13,256]{3,2,1,0:T(8,128)S(1)}, f32[1,8,13,256]{3,2,1,0:T(8,128)S(1)}, u32[]{:S(2)}, u32[]{:S(2)}) collective-permute-start(f32[1,8,13,256]{3,2,1,0:T(8,128)S(1)} %get-tuple-element.19), channel_id=1, source_target_pairs={{48,0},{96,48},{144,96},{192,144},{240,192},{288,240},{336,288},{3... | collective-permute-start | bytes 319496 | tf_op jit(solution)/shard_map/ppermute | solution.py:24
  24.1 4.0 %collective-permute-start.2 = (bf16[6,1,128]{2,1,0:T(2,128)(2,1)S(1)}, bf16[6,1,128]{2,1,0:T(2,128)(2,1)S(1)}, u32[]{:S(2)}, u32[]{:S(2)}) collective-permute-start(bf16[6,1,128]{2,1,0:T(2,128)(2,1)S(1)} %get-tuple-element.24), channel_id=1, source_target_pairs={{0,1},{1,2},{2,3},{3,4},{4,5},{5,6},{6,7},{7,8},{8,9},{9,10},{10,1... | collective-permute-start | bytes 4616 | tf_op jit(solution)/shard_map/ppermute | solution.py:22
  28.1 12.6 %collective-permute-start.3 = (bf16[6,1,128]{2,1,0:T(2,128)(2,1)S(1)}, bf16[6,1,128]{2,1,0:T(2,128)(2,1)S(1)}, u32[]{:S(2)}, u32[]{:S(2)}) collective-permute-start(bf16[6,1,128]{2,1,0:T(2,128)(2,1)S(1)} %get-tuple-element.25), channel_id=1, source_target_pairs={{1,0},{2,1},{3,2},{4,3},{5,4},{6,5},{7,6},{8,7},{9,8},{10,9},{11,1... | collective-permute-start | bytes 4616 | tf_op jit(solution)/shard_map/ppermute | solution.py:24
  40.8 0.7 collective-permute-done.3
  42.9 1.9 %collective-permute-start.7 = (f32[4,1,3,169]{3,1,0,2:T(1,128)S(1)}, f32[4,1,3,169]{3,1,0,2:T(1,128)S(1)}, u32[]{:S(2)}, u32[]{:S(2)}) collective-permute-start(f32[4,1,3,169]{3,1,0,2:T(1,128)S(1)} %pad_maximum_fusion.35), channel_id=1, source_target_pairs={{0,1},{1,2},{2,3},{3,4},{4,5},{5,6},{6,7},{7,8},{8,9},{9,10},{10,1... | collective-permute-start | bytes 24344 | tf_op jit(solution)/shard_map/ppermute | solution.py:33
  45.5 6.0 %collective-permute-done.7 = f32[4,1,3,169]{3,1,0,2:T(1,128)S(1)} collective-permute-done((f32[4,1,3,169]{3,1,0,2:T(1,128)S(1)}, f32[4,1,3,169]{3,1,0,2:T(1,128)S(1)}, u32[]{:S(2)}, u32[]{:S(2)}) %collective-permute-start.7) | collective-permute-done | bytes 8144 | tf_op jit(solution)/shard_map/ppermute | solution.py:33
  51.5 11.7 %collective-permute-start.9 = (f32[1,9,3,169]{3,1,0,2:T(8,128)S(1)}, f32[1,9,3,169]{3,1,0,2:T(8,128)S(1)}, u32[]{:S(2)}, u32[]{:S(2)}) collective-permute-start(f32[1,9,3,169]{3,1,0,2:T(8,128)S(1)} %pad_maximum_fusion.24), channel_id=1, source_target_pairs={{0,48},{48,96},{96,144},{144,192},{192,240},{240,288},{288,336},{3... | collective-permute-start | bytes 54764 | tf_op jit(solution)/shard_map/ppermute | solution.py:33
  63.2 1.5 %fusion.52 = f32[4,8,13,256]{3,2,1,0:T(8,128)} fusion(f32[4,8,13,256]{3,1,2,0:T(8,128)S(1)} %copy-done.1, f32[4,8,13,13]{3,2,1,0:T(8,128)S(1)} %reshape.16, f32[4,8,13,13]{2,3,1,0:T(8,128)S(1)} %copy.28), kind=kOutput, calls=%fused_computation.84 | convolution fusion | flops 16624192 | bytes 895232 | tf_op jit(solution)/shard_map/xyab,xybv->xyav/dot_general | solution.py:41
  65.9 3.6 %collective-permute-start.6 = (f32[6,1,13,256]{3,2,1,0:T(8,128)S(1)}, f32[6,1,13,256]{3,2,1,0:T(8,128)S(1)}, u32[]{:S(2)}, u32[]{:S(2)}) collective-permute-start(f32[6,1,13,256]{3,2,1,0:T(8,128)S(1)} %get-tuple-element.13), channel_id=1, source_target_pairs={{1,0},{2,1},{3,2},{4,3},{5,4},{6,5},{7,6},{8,7},{9,8},{10,9},{11,1... | collective-permute-start | bytes 239624 | tf_op jit(solution)/shard_map/ppermute | solution.py:24
  69.5 1.9 %collective-permute-start.8 = (f32[6,1,13,256]{3,2,1,0:T(8,128)S(1)}, f32[6,1,13,256]{3,2,1,0:T(8,128)S(1)}, u32[]{:S(2)}, u32[]{:S(2)}) collective-permute-start(f32[6,1,13,256]{3,2,1,0:T(8,128)S(1)} %get-tuple-element.14), channel_id=1, source_target_pairs={{0,1},{1,2},{2,3},{3,4},{4,5},{5,6},{6,7},{7,8},{8,9},{9,10},{10,1... | collective-permute-start | bytes 239624 | tf_op jit(solution)/shard_map/ppermute | solution.py:22
  71.5 0.6 fusion.47
  72.1 0.6 fusion.49
  73.1 0.6 convolution_add_fusion.5
  73.7 0.6 fusion.45
  74.3 4.5 %collective-permute-done.8 = f32[6,1,13,256]{3,2,1,0:T(8,128)S(1)} collective-permute-done((f32[6,1,13,256]{3,2,1,0:T(8,128)S(1)}, f32[6,1,13,256]{3,2,1,0:T(8,128)S(1)}, u32[]{:S(2)}, u32[]{:S(2)}) %collective-permute-start.8) | collective-permute-done | bytes 79904 | tf_op jit(solution)/shard_map/ppermute | solution.py:22
  78.8 0.6 fusion.43
  79.4 0.9 broadcast_multiply_fusion
  80.3 10.9 %collective-permute-start.10 = (f32[1,8,13,256]{3,2,1,0:T(8,128)S(1)}, f32[1,8,13,256]{3,2,1,0:T(8,128)S(1)}, u32[]{:S(2)}, u32[]{:S(2)}) collective-permute-start(f32[1,8,13,256]{3,2,1,0:T(8,128)S(1)} %get-tuple-element.17), channel_id=1, source_target_pairs={{0,48},{48,96},{96,144},{144,192},{192,240},{240,288},{288,336},{3... | collective-permute-start | bytes 319496 | tf_op jit(solution)/shard_map/ppermute | solution.py:22
  91.2 1.9 %collective-permute-start.11 = (f32[1,8,13,256]{3,2,1,0:T(8,128)S(1)}, f32[1,8,13,256]{3,2,1,0:T(8,128)S(1)}, u32[]{:S(2)}, u32[]{:S(2)}) collective-permute-start(f32[1,8,13,256]{3,2,1,0:T(8,128)S(1)} %get-tuple-element.18), channel_id=1, source_target_pairs={{48,0},{96,48},{144,96},{192,144},{240,192},{288,240},{336,288},{3... | collective-permute-start | bytes 319496 | tf_op jit(solution)/shard_map/ppermute | solution.py:24
  93.2 0.6 fusion.103
  93.8 9.7 %collective-permute-done.11 = f32[1,8,13,256]{3,2,1,0:T(8,128)S(1)} collective-permute-done((f32[1,8,13,256]{3,2,1,0:T(8,128)S(1)}, f32[1,8,13,256]{3,2,1,0:T(8,128)S(1)}, u32[]{:S(2)}, u32[]{:S(2)}) %collective-permute-start.11) | collective-permute-done | bytes 106528 | tf_op jit(solution)/shard_map/ppermute | solution.py:24
  103.6 1.9 %collective-permute-start.12 = (f32[6,1,13,256]{3,2,1,0:T(8,128)S(1)}, f32[6,1,13,256]{3,2,1,0:T(8,128)S(1)}, u32[]{:S(2)}, u32[]{:S(2)}) collective-permute-start(f32[6,1,13,256]{3,2,1,0:T(8,128)S(1)} %get-tuple-element.11), channel_id=1, source_target_pairs={{1,0},{2,1},{3,2},{4,3},{5,4},{6,5},{7,6},{8,7},{9,8},{10,9},{11,1... | collective-permute-start | bytes 239624 | tf_op jit(solution)/shard_map/ppermute | solution.py:24
  105.5 3.5 %collective-permute-start.13 = (f32[6,1,13,256]{3,2,1,0:T(8,128)S(1)}, f32[6,1,13,256]{3,2,1,0:T(8,128)S(1)}, u32[]{:S(2)}, u32[]{:S(2)}) collective-permute-start(f32[6,1,13,256]{3,2,1,0:T(8,128)S(1)} %get-tuple-element.12), channel_id=1, source_target_pairs={{0,1},{1,2},{2,3},{3,4},{4,5},{5,6},{6,7},{7,8},{8,9},{9,10},{10,1... | collective-permute-start | bytes 239624 | tf_op jit(solution)/shard_map/ppermute | solution.py:22
  109.0 0.6 fusion.39
  109.6 0.6 fusion.37
  110.3 4.5 %collective-permute-done.13 = f32[6,1,13,256]{3,2,1,0:T(8,128)S(1)} collective-permute-done((f32[6,1,13,256]{3,2,1,0:T(8,128)S(1)}, f32[6,1,13,256]{3,2,1,0:T(8,128)S(1)}, u32[]{:S(2)}, u32[]{:S(2)}) %collective-permute-start.13) | collective-permute-done | bytes 79904 | tf_op jit(solution)/shard_map/ppermute | solution.py:22
  115.6 0.6 convolution_add_fusion.3
  116.2 0.7 fusion.33
  116.8 1.0 fusion.13
  117.8 3.2 %collective-permute-start.14 = (f32[1,8,13,256]{3,2,1,0:T(8,128)S(1)}, f32[1,8,13,256]{3,2,1,0:T(8,128)S(1)}, u32[]{:S(2)}, u32[]{:S(2)}) collective-permute-start(f32[1,8,13,256]{3,2,1,0:T(8,128)S(1)} %get-tuple-element.15), channel_id=1, source_target_pairs={{0,48},{48,96},{96,144},{144,192},{192,240},{240,288},{288,336},{3... | collective-permute-start | bytes 319496 | tf_op jit(solution)/shard_map/ppermute | solution.py:22
  121.1 1.9 %collective-permute-start.15 = (f32[1,8,13,256]{3,2,1,0:T(8,128)S(1)}, f32[1,8,13,256]{3,2,1,0:T(8,128)S(1)}, u32[]{:S(2)}, u32[]{:S(2)}) collective-permute-start(f32[1,8,13,256]{3,2,1,0:T(8,128)S(1)} %get-tuple-element.16), channel_id=1, source_target_pairs={{48,0},{96,48},{144,96},{192,144},{240,192},{288,240},{336,288},{3... | collective-permute-start | bytes 319496 | tf_op jit(solution)/shard_map/ppermute | solution.py:24
  123.0 0.6 fusion.104
  123.6 9.8 %collective-permute-done.15 = f32[1,8,13,256]{3,2,1,0:T(8,128)S(1)} collective-permute-done((f32[1,8,13,256]{3,2,1,0:T(8,128)S(1)}, f32[1,8,13,256]{3,2,1,0:T(8,128)S(1)}, u32[]{:S(2)}, u32[]{:S(2)}) %collective-permute-start.15) | collective-permute-done | bytes 106528 | tf_op jit(solution)/shard_map/ppermute | solution.py:24
  133.4 1.9 %collective-permute-start.16 = (f32[6,1,13,256]{3,2,1,0:T(8,128)S(1)}, f32[6,1,13,256]{3,2,1,0:T(8,128)S(1)}, u32[]{:S(2)}, u32[]{:S(2)}) collective-permute-start(f32[6,1,13,256]{3,2,1,0:T(8,128)S(1)} %get-tuple-element.7), channel_id=1, source_target_pairs={{1,0},{2,1},{3,2},{4,3},{5,4},{6,5},{7,6},{8,7},{9,8},{10,9},{11,1... | collective-permute-start | bytes 239624 | tf_op jit(solution)/shard_map/ppermute | solution.py:24
  135.3 3.4 %collective-permute-start.17 = (f32[6,1,13,256]{3,2,1,0:T(8,128)S(1)}, f32[6,1,13,256]{3,2,1,0:T(8,128)S(1)}, u32[]{:S(2)}, u32[]{:S(2)}) collective-permute-start(f32[6,1,13,256]{3,2,1,0:T(8,128)S(1)} %get-tuple-element.8), channel_id=1, source_target_pairs={{0,1},{1,2},{2,3},{3,4},{4,5},{5,6},{6,7},{7,8},{8,9},{9,10},{10,1... | collective-permute-start | bytes 239624 | tf_op jit(solution)/shard_map/ppermute | solution.py:22
  138.7 0.6 fusion.29
  139.3 0.6 fusion.27
  139.9 4.7 %collective-permute-done.17 = f32[6,1,13,256]{3,2,1,0:T(8,128)S(1)} collective-permute-done((f32[6,1,13,256]{3,2,1,0:T(8,128)S(1)}, f32[6,1,13,256]{3,2,1,0:T(8,128)S(1)}, u32[]{:S(2)}, u32[]{:S(2)}) %collective-permute-start.17) | collective-permute-done | bytes 79904 | tf_op jit(solution)/shard_map/ppermute | solution.py:22
  144.8 0.6 fusion.25
  146.0 0.7 fusion.23
  146.7 0.8 fusion.6
  147.5 1.0 copy.46
  (65 shorter events, 5.4 us)
Async XLA Ops:
  0.0 42.4 %copy-start = (bf16[128,169]{0,1:T(8,128)(2,1)S(1)}, bf16[128,169]{0,1:T(8,128)(2,1)}, u32[]{:S(2)}) copy-start(bf16[128,169]{0,1:T(8,128)(2,1)} %param.14) | copy-start | bytes 129796
  0.7 23.3 %collective-permute-start = (bf16[1,8,128]{2,1,0:T(8,128)(2,1)S(1)}, bf16[1,8,128]{2,1,0:T(8,128)(2,1)S(1)}, u32[]{:S(2)}, u32[]{:S(2)}) collective-permute-start(bf16[1,8,128]{2,1,0:T(8,128)(2,1)S(1)} %get-tuple-element.27), channel_id=1, source_target_pairs={{0,48},{48,96},{96,144},{144,192},{192,240},{240,288},{288,336},{3... | collective-permute-start | bytes 6152 | tf_op jit(solution)/shard_map/ppermute | solution.py:22
  8.6 15.4 %collective-permute-start.1 = (bf16[1,8,128]{2,1,0:T(8,128)(2,1)S(1)}, bf16[1,8,128]{2,1,0:T(8,128)(2,1)S(1)}, u32[]{:S(2)}, u32[]{:S(2)}) collective-permute-start(bf16[1,8,128]{2,1,0:T(8,128)(2,1)S(1)} %get-tuple-element.26), channel_id=1, source_target_pairs={{48,0},{96,48},{144,96},{192,144},{240,192},{288,240},{336,288},{3... | collective-permute-start | bytes 6152 | tf_op jit(solution)/shard_map/ppermute | solution.py:24
  11.7 12.3 %copy-start.5 = (s32[4,8,3]{1,0,2:T(4,128)S(1)}, s32[4,8,3]{1,0,2:T(4,128)}, u32[]{:S(2)}) copy-start(s32[4,8,3]{1,0,2:T(4,128)} %param.9) | copy-start | bytes 1156
  12.4 53.2 %collective-permute-start.4 = (f32[1,8,13,256]{3,2,1,0:T(8,128)}, f32[1,8,13,256]{3,2,1,0:T(8,128)S(1)}, u32[]{:S(2)}, u32[]{:S(2)}) collective-permute-start(f32[1,8,13,256]{3,2,1,0:T(8,128)} %get-tuple-element.20), channel_id=1, source_target_pairs={{0,48},{48,96},{96,144},{144,192},{192,240},{240,288},{288,336},{3... | collective-permute-start | bytes 319496 | tf_op jit(solution)/shard_map/ppermute | solution.py:22
  22.1 2.0 %copy-start.4 = (bf16[4,8,128]{2,1,0:T(8,128)(2,1)S(1)}, bf16[4,8,128]{2,1,0:T(8,128)(2,1)}, u32[]{:S(2)}) copy-start(bf16[4,8,128]{2,1,0:T(8,128)(2,1)} %param.8) | copy-start | bytes 24580
  22.1 43.8 %collective-permute-start.5 = (f32[1,8,13,256]{3,2,1,0:T(8,128)S(1)}, f32[1,8,13,256]{3,2,1,0:T(8,128)S(1)}, u32[]{:S(2)}, u32[]{:S(2)}) collective-permute-start(f32[1,8,13,256]{3,2,1,0:T(8,128)S(1)} %get-tuple-element.19), channel_id=1, source_target_pairs={{48,0},{96,48},{144,96},{192,144},{240,192},{288,240},{336,288},{3... | collective-permute-start | bytes 319496 | tf_op jit(solution)/shard_map/ppermute | solution.py:24
  24.1 16.6 %copy-start.6 = (f32[4,128]{1,0:T(4,128)S(1)}, f32[4,128]{1,0:T(4,128)}, u32[]{:S(2)}) copy-start(f32[4,128]{1,0:T(4,128)} %param.13) | copy-start | bytes 6148
  24.1 16.6 %collective-permute-start.2 = (bf16[6,1,128]{2,1,0:T(2,128)(2,1)S(1)}, bf16[6,1,128]{2,1,0:T(2,128)(2,1)S(1)}, u32[]{:S(2)}, u32[]{:S(2)}) collective-permute-start(bf16[6,1,128]{2,1,0:T(2,128)(2,1)S(1)} %get-tuple-element.24), channel_id=1, source_target_pairs={{0,1},{1,2},{2,3},{3,4},{4,5},{5,6},{6,7},{7,8},{8,9},{9,10},{10,1... | collective-permute-start | bytes 4616 | tf_op jit(solution)/shard_map/ppermute | solution.py:22
  28.1 13.3 %collective-permute-start.3 = (bf16[6,1,128]{2,1,0:T(2,128)(2,1)S(1)}, bf16[6,1,128]{2,1,0:T(2,128)(2,1)S(1)}, u32[]{:S(2)}, u32[]{:S(2)}) collective-permute-start(bf16[6,1,128]{2,1,0:T(2,128)(2,1)S(1)} %get-tuple-element.25), channel_id=1, source_target_pairs={{1,0},{2,1},{3,2},{4,3},{5,4},{6,5},{7,6},{8,7},{9,8},{10,9},{11,1... | collective-permute-start | bytes 4616 | tf_op jit(solution)/shard_map/ppermute | solution.py:24
  40.7 0.8 copy-start.7
  40.7 0.8 copy-start.8
  41.5 0.8 copy-start.3
  42.9 8.6 %collective-permute-start.7 = (f32[4,1,3,169]{3,1,0,2:T(1,128)S(1)}, f32[4,1,3,169]{3,1,0,2:T(1,128)S(1)}, u32[]{:S(2)}, u32[]{:S(2)}) collective-permute-start(f32[4,1,3,169]{3,1,0,2:T(1,128)S(1)} %pad_maximum_fusion.35), channel_id=1, source_target_pairs={{0,1},{1,2},{2,3},{3,4},{4,5},{5,6},{6,7},{7,8},{8,9},{9,10},{10,1... | collective-permute-start | bytes 24344 | tf_op jit(solution)/shard_map/ppermute | solution.py:33
  45.0 18.2 %copy-start.1 = (f32[4,8,13,256]{3,1,2,0:T(8,128)S(1)}, f32[4,8,13,256]{3,1,2,0:T(8,128)}, u32[]{:S(2)}) copy-start(f32[4,8,13,256]{3,1,2,0:T(8,128)} %param.15) | copy-start | bytes 1277956
  51.5 13.7 %collective-permute-start.9 = (f32[1,9,3,169]{3,1,0,2:T(8,128)S(1)}, f32[1,9,3,169]{3,1,0,2:T(8,128)S(1)}, u32[]{:S(2)}, u32[]{:S(2)}) collective-permute-start(f32[1,9,3,169]{3,1,0,2:T(8,128)S(1)} %pad_maximum_fusion.24), channel_id=1, source_target_pairs={{0,48},{48,96},{96,144},{144,192},{192,240},{240,288},{288,336},{3... | collective-permute-start | bytes 54764 | tf_op jit(solution)/shard_map/ppermute | solution.py:33
  65.9 6.8 %collective-permute-start.6 = (f32[6,1,13,256]{3,2,1,0:T(8,128)S(1)}, f32[6,1,13,256]{3,2,1,0:T(8,128)S(1)}, u32[]{:S(2)}, u32[]{:S(2)}) collective-permute-start(f32[6,1,13,256]{3,2,1,0:T(8,128)S(1)} %get-tuple-element.13), channel_id=1, source_target_pairs={{1,0},{2,1},{3,2},{4,3},{5,4},{6,5},{7,6},{8,7},{9,8},{10,9},{11,1... | collective-permute-start | bytes 239624 | tf_op jit(solution)/shard_map/ppermute | solution.py:24
  69.5 9.3 %collective-permute-start.8 = (f32[6,1,13,256]{3,2,1,0:T(8,128)S(1)}, f32[6,1,13,256]{3,2,1,0:T(8,128)S(1)}, u32[]{:S(2)}, u32[]{:S(2)}) collective-permute-start(f32[6,1,13,256]{3,2,1,0:T(8,128)S(1)} %get-tuple-element.14), channel_id=1, source_target_pairs={{0,1},{1,2},{2,3},{3,4},{4,5},{5,6},{6,7},{7,8},{8,9},{9,10},{10,1... | collective-permute-start | bytes 239624 | tf_op jit(solution)/shard_map/ppermute | solution.py:22
  72.1 1.0 copy-start.2
  80.3 13.4 %collective-permute-start.10 = (f32[1,8,13,256]{3,2,1,0:T(8,128)S(1)}, f32[1,8,13,256]{3,2,1,0:T(8,128)S(1)}, u32[]{:S(2)}, u32[]{:S(2)}) collective-permute-start(f32[1,8,13,256]{3,2,1,0:T(8,128)S(1)} %get-tuple-element.17), channel_id=1, source_target_pairs={{0,48},{48,96},{96,144},{144,192},{192,240},{240,288},{288,336},{3... | collective-permute-start | bytes 319496 | tf_op jit(solution)/shard_map/ppermute | solution.py:22
  91.2 12.3 %collective-permute-start.11 = (f32[1,8,13,256]{3,2,1,0:T(8,128)S(1)}, f32[1,8,13,256]{3,2,1,0:T(8,128)S(1)}, u32[]{:S(2)}, u32[]{:S(2)}) collective-permute-start(f32[1,8,13,256]{3,2,1,0:T(8,128)S(1)} %get-tuple-element.18), channel_id=1, source_target_pairs={{48,0},{96,48},{144,96},{192,144},{240,192},{288,240},{336,288},{3... | collective-permute-start | bytes 319496 | tf_op jit(solution)/shard_map/ppermute | solution.py:24
  103.6 6.7 %collective-permute-start.12 = (f32[6,1,13,256]{3,2,1,0:T(8,128)S(1)}, f32[6,1,13,256]{3,2,1,0:T(8,128)S(1)}, u32[]{:S(2)}, u32[]{:S(2)}) collective-permute-start(f32[6,1,13,256]{3,2,1,0:T(8,128)S(1)} %get-tuple-element.11), channel_id=1, source_target_pairs={{1,0},{2,1},{3,2},{4,3},{5,4},{6,5},{7,6},{8,7},{9,8},{10,9},{11,1... | collective-permute-start | bytes 239624 | tf_op jit(solution)/shard_map/ppermute | solution.py:24
  105.5 9.3 %collective-permute-start.13 = (f32[6,1,13,256]{3,2,1,0:T(8,128)S(1)}, f32[6,1,13,256]{3,2,1,0:T(8,128)S(1)}, u32[]{:S(2)}, u32[]{:S(2)}) collective-permute-start(f32[6,1,13,256]{3,2,1,0:T(8,128)S(1)} %get-tuple-element.12), channel_id=1, source_target_pairs={{0,1},{1,2},{2,3},{3,4},{4,5},{5,6},{6,7},{7,8},{8,9},{9,10},{10,1... | collective-permute-start | bytes 239624 | tf_op jit(solution)/shard_map/ppermute | solution.py:22
  117.8 5.7 %collective-permute-start.14 = (f32[1,8,13,256]{3,2,1,0:T(8,128)S(1)}, f32[1,8,13,256]{3,2,1,0:T(8,128)S(1)}, u32[]{:S(2)}, u32[]{:S(2)}) collective-permute-start(f32[1,8,13,256]{3,2,1,0:T(8,128)S(1)} %get-tuple-element.15), channel_id=1, source_target_pairs={{0,48},{48,96},{96,144},{144,192},{192,240},{240,288},{288,336},{3... | collective-permute-start | bytes 319496 | tf_op jit(solution)/shard_map/ppermute | solution.py:22
  121.1 12.3 %collective-permute-start.15 = (f32[1,8,13,256]{3,2,1,0:T(8,128)S(1)}, f32[1,8,13,256]{3,2,1,0:T(8,128)S(1)}, u32[]{:S(2)}, u32[]{:S(2)}) collective-permute-start(f32[1,8,13,256]{3,2,1,0:T(8,128)S(1)} %get-tuple-element.16), channel_id=1, source_target_pairs={{48,0},{96,48},{144,96},{192,144},{240,192},{288,240},{336,288},{3... | collective-permute-start | bytes 319496 | tf_op jit(solution)/shard_map/ppermute | solution.py:24
  133.4 6.5 %collective-permute-start.16 = (f32[6,1,13,256]{3,2,1,0:T(8,128)S(1)}, f32[6,1,13,256]{3,2,1,0:T(8,128)S(1)}, u32[]{:S(2)}, u32[]{:S(2)}) collective-permute-start(f32[6,1,13,256]{3,2,1,0:T(8,128)S(1)} %get-tuple-element.7), channel_id=1, source_target_pairs={{1,0},{2,1},{3,2},{4,3},{5,4},{6,5},{7,6},{8,7},{9,8},{10,9},{11,1... | collective-permute-start | bytes 239624 | tf_op jit(solution)/shard_map/ppermute | solution.py:24
  135.3 9.3 %collective-permute-start.17 = (f32[6,1,13,256]{3,2,1,0:T(8,128)S(1)}, f32[6,1,13,256]{3,2,1,0:T(8,128)S(1)}, u32[]{:S(2)}, u32[]{:S(2)}) collective-permute-start(f32[6,1,13,256]{3,2,1,0:T(8,128)S(1)} %get-tuple-element.8), channel_id=1, source_target_pairs={{0,1},{1,2},{2,3},{3,4},{4,5},{5,6},{6,7},{7,8},{8,9},{9,10},{10,1... | collective-permute-start | bytes 239624 | tf_op jit(solution)/shard_map/ppermute | solution.py:22
where the time goes:
time: 149 us
  starting transfers between devices  85.8 us (58%)
  waiting for transfers between devices  39.8 us (27%)
  matrix products  15.4 us (10%)
  local copies, waits for them, and re-layouts  6.19 us (4%)
    ppermute x8, starting transfers between devices, with_halo(): lax.ppermute(tail, axis, [(i, (i + 1) % count) for i in range(count)])  44.5 us
    ppermute x8, starting transfers between devices, with_halo(): lax.ppermute(head, axis, [((i + 1) % count, i) for i in range(count)])  27.8 us
    ppermute x8, waiting for transfers between devices, with_halo(): lax.ppermute(head, axis, [((i + 1) % count, i) for i in range(count)])  20.2 us
    dot_general x21, matrix products, contract(): jnp.einsum('xyab,xybv->xyav', blocks, vectors_in, precision=lax.Precision...  14.4 us
    ppermute x8, waiting for transfers between devices, with_halo(): lax.ppermute(tail, axis, [(i, (i + 1) % count) for i in range(count)])  13.6 us
    ppermute x2, starting transfers between devices, shifted(): lax.ppermute(x, axis, [(i, (i + by) % length) for i in range(length)])  13.6 us
    ppermute x2, waiting for transfers between devices, shifted(): lax.ppermute(x, axis, [(i, (i + by) % length) for i in range(length)])  6 us
  transfers between devices with their start and end apart: 18, of which 7 were waited for; matrix products, arithmetic and copies ran while one was open for 8% of the time, Pallas kernels for 0%

commit v1 on v0

v1 whole, which is shorter than its diff:
```python
import functools

import jax
import jax.numpy as jnp
from jax import lax
from jax.experimental import pallas as pl
from jax.experimental.pallas import tpu as pltpu
from jax.sharding import PartitionSpec as P

ORBITALS = 13
PAD = 16
CENTRE = 4.0
HALF_WIDTH = 24.0
MESH = pl.DeviceIdType.MESH
F32 = jnp.float32
BF16 = jnp.bfloat16

SIDES = ((0, 1), (1, 1), (-1, 1), (0, -1), (-1, -1), (1, -1), (1, 0), (-1, 0))
BLOCKS = (
    (-1, -1, 0, 2, True),
    (-1, 0, 1, 1, True),
    (0, -1, 5, 0, True),
    (0, 0, 6, 3, False),
    (0, 1, 7, 0, False),
    (1, 0, 11, 1, False),
    (1, 1, 12, 2, False),
)


def span(step, size, width):
    if step > 0:
        return slice(size - width, size), slice(3 - width, 3)
    if step < 0:
        return slice(0, width), slice(3 + size, 3 + size + width)
    return slice(0, size), slice(3, 3 + size)


def iota(shape, axis):
    return lax.broadcasted_iota(jnp.int32, shape, axis)


def place_weights(w_block, base, transposed):
    lane = iota((ORBITALS * ORBITALS, 256), 1)
    source = iota((ORBITALS * ORBITALS, 256), 0)
    b = lane & 15
    a = 8 * (lane >> 7) + ((base - ((lane >> 4) & 7)) & 7)
    entry = b * ORBITALS + a if transposed else a * ORBITALS + b
    chosen = (source == entry) & (a < ORBITALS) & (b < ORBITALS)
    return jnp.dot(w_block, chosen.astype(F32).astype(BF16), preferred_element_type=F32).astype(BF16)


def kernel(
    features_hbm, mask_hbm, update_hbm, atom_hbm, pair_hbm, bias_hbm, block_hbm, trial_hbm,
    out_ref,
    features_in, mask_in, w_update, w_atom, w_pair, bias, w_block, trial,
    patches, mask_wide, x_hi, x_lo, y_hi, z_hi, y, z, placed, gather, select,
    self_part, pair_part, masks, blocks, h_full, h_hi, h_lo,
    load_sem, send_f, recv_f, send_x, recv_x,
):
    px, py = lax.axis_index("px"), lax.axis_index("py")
    nx, ny = lax.axis_size("px"), lax.axis_size("py")

    def device(side):
        return (lax.rem(px + side[0] + nx, nx), lax.rem(py + side[1] + ny, ny))

    barrier = pltpu.get_barrier_semaphore()
    for side in SIDES:
        pl.semaphore_signal(barrier, inc=1, device_id=device(side), device_id_type=MESH)

    loads = []
    pairs = (
        (trial_hbm, trial), (features_hbm, features_in), (mask_hbm, mask_in), (update_hbm, w_update),
        (atom_hbm, w_atom), (pair_hbm, w_pair), (bias_hbm, bias), (block_hbm, w_block),
    )
    for i, (source, target) in enumerate(pairs):
        copy = pltpu.make_async_copy(source, target, load_sem.at[i])
        copy.start()
        loads.append(copy)

    for rows, columns in ((0, slice(11, 14)), (slice(1, 3), 13), (9, slice(0, 3)), (slice(7, 9), 0)):
        x_hi[rows, columns] = jnp.zeros_like(x_hi[rows, columns])
    x_lo[...] = jnp.zeros_like(x_lo)
    mask_wide[...] = jnp.zeros_like(mask_wide)
    trial_pad = jnp.zeros((8, PAD - ORBITALS, 256), F32)
    for i in range(1, 3):
        loads[i].wait()
    patches[4, :, :128] = features_in[...].astype(F32).reshape(32, 128).astype(BF16)
    mask_wide[:, :3] = mask_in[...].astype(F32).reshape(32, 3)
    patches[4, :, 128:] = mask_wide[...].astype(BF16)
    loads[0].wait()
    for r in range(4):
        wide = jnp.concatenate([trial[r], trial_pad], axis=1)
        high = wide.astype(BF16)
        x_hi[3 + r, 3:11] = high
        x_lo[3 + r, 3:11] = (wide - high.astype(F32)).astype(BF16)

    pl.semaphore_wait(barrier, len(SIDES))

    feature_copies, vector_copies = [], []
    for i, side in enumerate(SIDES):
        mine = (1 - side[0]) * 3 + (1 - side[1])
        copy = pltpu.make_async_remote_copy(
            src_ref=patches.at[4], dst_ref=patches.at[mine], send_sem=send_f.at[i], recv_sem=recv_f.at[i],
            device_id=device(side), device_id_type=MESH,
        )
        copy.start()
        feature_copies.append(copy)
    for i, side in enumerate(SIDES):
        width = 2 if side[0] * side[1] < 0 else 3
        from_r, to_r = span(side[0], 4, width)
        from_c, to_c = span(side[1], 8, width)
        shift = lambda s: slice(3 + s.start, 3 + s.stop)
        copy = pltpu.make_async_remote_copy(
            src_ref=x_hi.at[shift(from_r), shift(from_c)], dst_ref=x_hi.at[to_r, to_c],
            send_sem=send_x.at[i], recv_sem=recv_x.at[i], device_id=device(side), device_id_type=MESH,
        )
        copy.start()
        vector_copies.append(copy)

    for i in range(3, 8):
        loads[i].wait()
    for i, (_, _, base, slot, transposed) in enumerate(BLOCKS):
        placed[i] = place_weights(w_block[...], base, transposed)
    placed[7] = place_weights(w_block[...], BLOCKS[3][2], True)
    y_hi[...] = jnp.zeros_like(y_hi)
    z_hi[...] = jnp.zeros_like(z_hi)
    h_full[...] = jnp.zeros_like(h_full)
    point = iota((224, 1), 0)
    cell = iota((1, 288), 1)
    patch = cell >> 5
    patch_row = (patch >= 3).astype(jnp.int32) + (patch >= 6).astype(jnp.int32)
    down = (patch_row * 4 - 4 + ((cell >> 3) & 3)) - ((point & 15) - 3)
    right = ((patch - 3 * patch_row) * 8 - 8 + (cell & 7)) - ((point >> 4) - 3)
    same = (down == 0) & (right == 0)
    near = (jnp.abs(down) <= 1) & (jnp.abs(right) <= 1) & (down + right != 0) | (
        (down == right) & (jnp.abs(down) == 1)
    )
    select[...] = same.astype(F32).astype(BF16)
    gather[...] = near.astype(F32).astype(BF16)

    for copy in feature_copies:
        copy.wait_recv()

    around = patches[...].reshape(288, 256)
    picked = jnp.dot(select[...], around, preferred_element_type=F32)
    gathered = jnp.dot(gather[...], around[:, :128], preferred_element_type=F32)
    own = picked[:, :128]
    update = jax.nn.silu(jnp.dot(gathered.astype(BF16), w_update[...], preferred_element_type=F32))
    refined = (own + update).astype(BF16)
    self_part[...] = jnp.dot(refined, w_atom[...], preferred_element_type=F32).reshape(14, 16, 128)
    pair_part[...] = jnp.dot(own.astype(BF16), w_pair[...], preferred_element_type=F32).reshape(14, 16, 128)
    masks[...] = picked[:, 128:].reshape(14, 16, 128)

    for i, (dr, dc, base, slot, transposed) in enumerate(BLOCKS):
        r0, c0 = (1 + dr, 1 + dc) if transposed else (1, 1)
        r1, c1 = (1, 1) if transposed else (1 + dr, 1 + dc)
        message = jax.nn.silu(
            self_part[c0 : c0 + 12, r0 : r0 + 8] + pair_part[c1 : c1 + 12, r1 : r1 + 8] + bias[slot : slot + 1]
        )
        if slot < 3:
            message = message * masks[c0 : c0 + 12, r0 : r0 + 8, slot : slot + 1]
        message = message.astype(BF16).reshape(96, 128)
        block = jnp.dot(message, placed[i], preferred_element_type=F32)
        if slot == 3:
            block = 0.5 * (block + jnp.dot(message, placed[7], preferred_element_type=F32))
        blocks[i] = block.reshape(12, 8, 256)

    lane_slot = iota((8, 128), 1) >> 4

    def assemble(g, carry):
        for c in range(4):
            for a in range(ORBITALS):
                half = slice(128 * (a // 8), 128 * (a // 8) + 128)
                for part in range(2):
                    value = jnp.zeros((8, 128), F32)
                    for i, (_, _, base, _, _) in enumerate(BLOCKS):
                        if (base + c) // 8 == part:
                            value = jnp.where(lane_slot == (base - a) % 8, blocks[i, g * 4 + c, :, half], value)
                    turn = (c + a) * 16 % 128
                    if turn:
                        value = pltpu.roll(value, turn, axis=1)
                    h_full[part, pl.ds(g * 64 + c * 16 + a, 8, stride=192), :] = value
        return carry

    lax.fori_loop(0, 3, assemble, 0)

    def halves(r, carry):
        rows = pl.ds(pl.multiple_of(r * 192, 192), 192)
        full = jnp.concatenate([h_full[0, rows, :], h_full[1, rows, :]], axis=1)
        high = full.astype(BF16)
        h_hi[rows, :] = high
        h_lo[rows, :] = (full - high.astype(F32)).astype(BF16)
        return carry

    lax.fori_loop(0, 8, halves, 0)

    for copy in vector_copies:
        copy.wait_recv()

    def apply(vectors, r, g, first, last):
        c = 1 + 4 * g
        weights = jnp.concatenate(
            [
                vectors[r, c - 1 : c + 4].reshape(80, 256),
                vectors[r + 1, c - 1 : c + 5].reshape(96, 256),
                vectors[r + 2, c : c + 5].reshape(80, 256),
            ],
            axis=0,
        )
        rows = pl.ds(pl.multiple_of(r * 192 + g * 64 + first * 16, 16), (last - first) * 16)
        total = jnp.dot(h_hi[rows, :], weights, preferred_element_type=F32)
        total = total + jnp.dot(h_lo[rows, :], weights, preferred_element_type=F32)
        return total.reshape(last - first, PAD, 256)

    def start(r, c, n):
        return x_hi[r, c : c + n].astype(F32) + x_lo[r, c : c + n].astype(F32)

    def first_step(r, carry):
        for g in range(3):
            c = 1 + 4 * g
            value = (apply(x_hi, r, g, 0, 4) - CENTRE * start(r + 1, c, 4)) * (1.0 / HALF_WIDTH)
            y[r + 1, c : c + 4] = value
            y_hi[r + 1, c : c + 4] = value.astype(BF16)
        return carry

    lax.fori_loop(0, 8, first_step, 0)

    def second_step(r, carry):
        for g in range(3):
            c = 1 + 4 * g
            value = (apply(y_hi, r, g, 0, 4) - CENTRE * y[r + 1, c : c + 4]) * (2.0 / HALF_WIDTH)
            value = value - start(r + 1, c, 4)
            z_hi[r + 1, c : c + 4] = value.astype(BF16)
            z[r + 1, c : c + 4] = value
        return carry

    lax.fori_loop(1, 7, second_step, 0)

    def third_step(r, carry):
        for g, first, last in ((0, 2, 4), (1, 0, 4), (2, 0, 2)):
            c, n = 1 + 4 * g + first, last - first
            value = (apply(z_hi, r, g, first, last) - CENTRE * z[r + 1, c : c + n]) * (2.0 / HALF_WIDTH)
            value = value - y[r + 1, c : c + n]
            out_ref[r - 2, c - 3 : c - 3 + n] = value[:, :ORBITALS]
        return carry

    lax.fori_loop(2, 6, third_step, 0)

    for copy in feature_copies + vector_copies:
        copy.wait_send()


def per_device(features, pair_mask, w_update, w_atom, w_pair, slot_bias, w_block, trial):
    vectors = (10, 14, PAD, 256)
    sides = pltpu.SemaphoreType.DMA((len(SIDES),))
    return pl.pallas_call(
        kernel,
        name="filter",
        out_shape=jax.ShapeDtypeStruct(trial.shape, trial.dtype),
        in_specs=[pl.BlockSpec(memory_space=pl.ANY)] * 8,
        out_specs=pl.BlockSpec(memory_space=pltpu.VMEM),
        scratch_shapes=[
            pltpu.VMEM(features.shape, BF16),
            pltpu.VMEM(pair_mask.shape, jnp.int32),
            pltpu.VMEM(w_update.shape, BF16),
            pltpu.VMEM(w_atom.shape, BF16),
            pltpu.VMEM(w_pair.shape, BF16),
            pltpu.VMEM(slot_bias.shape, F32),
            pltpu.VMEM(w_block.shape, BF16),
            pltpu.VMEM(trial.shape, F32),
            pltpu.VMEM((9, 32, 256), BF16),
            pltpu.VMEM((32, 128), F32),
            pltpu.VMEM(vectors, BF16),
            pltpu.VMEM(vectors, BF16),
            pltpu.VMEM(vectors, BF16),
            pltpu.VMEM(vectors, BF16),
            pltpu.VMEM(vectors, F32),
            pltpu.VMEM(vectors, F32),
            pltpu.VMEM((8, 128, 256), BF16),
            pltpu.VMEM((224, 288), BF16),
            pltpu.VMEM((224, 288), BF16),
            pltpu.VMEM((14, 16, 128), F32),
            pltpu.VMEM((14, 16, 128), F32),
            pltpu.VMEM((14, 16, 128), F32),
            pltpu.VMEM((7, 12, 8, 256), F32),
            pltpu.VMEM((2, 1536, 128), F32),
            pltpu.VMEM((1536, 256), BF16),
            pltpu.VMEM((1536, 256), BF16),
            pltpu.SemaphoreType.DMA((8,)),
            sides,
            sides,
            sides,
            sides,
        ],
        compiler_params=pltpu.CompilerParams(
            collective_id=0, has_side_effects=True, vmem_limit_bytes=48 * 2**20
        ),
    )(features, pair_mask, w_update, w_atom, w_pair, slot_bias, w_block, trial)


def solution(mesh):
    return jax.shard_map(
        per_device,
        mesh=mesh,
        in_specs=(
            P("px", "py", None),
            P("px", "py", None),
            P(),
            P(),
            P(),
            P(),
            P(),
            P("px", "py", None, None),
        ),
        out_specs=P("px", "py", None, None),
        check_vma=False,
    )
```

time: 149 us -> 42.4 us (0.28)
  the two profiles are of different devices: /device:TPU:7 before, /device:TPU:8 now
where the time goes in v1:
time: 42.4 us; the launch traced here: 42.2 us
  Pallas kernels  38.2 us (90%)
  local copies, waits for them, and re-layouts  3.88 us (9%)
    pallas_call x1, Pallas kernels, per_device(): pl.pallas_call(kernel, name='filter', out_shape=jax.ShapeDtypeStruct(tria...  38.2 us
    unnamed x13, local copies, waits for them, and re-layouts  2.87 us
    pallas_call x1, local copies, waits for them, and re-layouts, per_device(): pl.pallas_call(kernel, name='filter', out_shape=jax.ShapeDtypeStruct(tria...  1.01 us

profile of v1, /device:TPU:8, one launch (start us, length us, event | category | flops | bytes accessed | tf_op | source)
XLA Modules:
  0.0 42.2 jit_solution(4035371308370207662)
XLA Ops:
  0.0 0.8 %copy.9.mask_hbm = s32[4,8,3]{2,1,0:T(8,128)S(1)} copy(s32[4,8,3]{1,0,2:T(4,128)} %param.9) | data formatting | bytes 768 | tf_op args[1]
  0.8 0.9 %copy.10.block_hbm = bf16[128,169]{1,0:T(8,128)(2,1)S(1)} copy(bf16[128,169]{0,1:T(8,128)(2,1)} %param.14) | data formatting | bytes 86528 | tf_op args[6]
  1.7 0.0 copy-start
  1.7 0.0 copy-start.1
  1.7 0.0 copy-start.2
  1.7 0.0 copy-start.3
  1.7 0.0 copy-start.4
  1.7 1.2 %copy.11.trial_hbm = f32[4,8,13,256]{3,2,1,0:T(8,128)S(1)} copy(f32[4,8,13,256]{3,1,2,0:T(8,128)} %param.15) | data formatting | bytes 851968 | tf_op args[7]
  2.9 0.0 copy-done
  2.9 0.0 copy-done.1
  2.9 0.0 copy-done.2
  2.9 0.0 copy-done.3
  3.0 0.0 copy-done.4
  3.0 38.2 %filter.1 = f32[4,8,13,256]{3,2,1,0:T(8,128)S(1)} custom-call(bf16[4,8,128]{2,1,0:T(8,128)(2,1)S(1)} %copy-done.3, s32[4,8,3]{2,1,0:T(8,128)S(1)} %copy.9.mask_hbm, bf16[128,128]{1,0:T(8,128)(2,1)S(1)} %copy-done, bf16[128,128]{1,0:T(8,128)(2,1)S(1)} %copy-done.1, bf16[128,128]{1,0:T(8,128)(2,1)S(1)} %copy-done.2, f32[4,128]{1,0:T(4,128)S(1)} %copy-done.4, ...), custom_call_target="tpu_custom_call" | custom-call | tf_op jit(solution)/shard_map/filter/pallas_call | solution.py:256
  41.2 1.0 %copy.12 = f32[4,8,13,256]{3,1,2,0:T(8,128)} copy(f32[4,8,13,256]{3,2,1,0:T(8,128)S(1)} %filter.1) | data formatting | bytes 851968 | tf_op jit(solution)/shard_map/filter/pallas_call | solution.py:256
Async XLA Ops:
  1.7 1.2 %copy-start = (bf16[128,128]{1,0:T(8,128)(2,1)S(1)}, bf16[128,128]{1,0:T(8,128)(2,1)}, u32[]{:S(2)}) copy-start(bf16[128,128]{1,0:T(8,128)(2,1)} %update_hbm.1) | copy-start | bytes 98308
  1.7 1.2 %copy-start.1 = (bf16[128,128]{1,0:T(8,128)(2,1)S(1)}, bf16[128,128]{1,0:T(8,128)(2,1)}, u32[]{:S(2)}) copy-start(bf16[128,128]{1,0:T(8,128)(2,1)} %atom_hbm.1) | copy-start | bytes 98308
  1.7 1.2 %copy-start.2 = (bf16[128,128]{1,0:T(8,128)(2,1)S(1)}, bf16[128,128]{1,0:T(8,128)(2,1)}, u32[]{:S(2)}) copy-start(bf16[128,128]{1,0:T(8,128)(2,1)} %pair_hbm.1) | copy-start | bytes 98308
  1.7 1.2 %copy-start.3 = (bf16[4,8,128]{2,1,0:T(8,128)(2,1)S(1)}, bf16[4,8,128]{2,1,0:T(8,128)(2,1)}, u32[]{:S(2)}) copy-start(bf16[4,8,128]{2,1,0:T(8,128)(2,1)} %features_hbm.1) | copy-start | bytes 24580
  1.7 1.2 %copy-start.4 = (f32[4,128]{1,0:T(4,128)S(1)}, f32[4,128]{1,0:T(4,128)}, u32[]{:S(2)}) copy-start(f32[4,128]{1,0:T(4,128)} %bias_hbm.1) | copy-start | bytes 6148

commit v2 on v1

--- a/solution.py
+++ b/solution.py
@@ -15,7 +15,11 @@
 F32 = jnp.float32
 BF16 = jnp.bfloat16
 
-SIDES = ((0, 1), (1, 1), (-1, 1), (0, -1), (-1, -1), (1, -1), (1, 0), (-1, 0))
+FORWARD = ((0, 1), (1, 1), (-1, 1))
+BACKWARD = ((0, -1), (-1, -1), (1, -1))
+ACROSS = ((1, 0), (-1, 0))
+SIDES = FORWARD + BACKWARD + ACROSS
+LAYERS = 12
 BLOCKS = (
     (-1, -1, 0, 2, True),
     (-1, 0, 1, 1, True),
@@ -46,16 +50,18 @@
     a = 8 * (lane >> 7) + ((base - ((lane >> 4) & 7)) & 7)
     entry = b * ORBITALS + a if transposed else a * ORBITALS + b
     chosen = (source == entry) & (a < ORBITALS) & (b < ORBITALS)
-    return jnp.dot(w_block, chosen.astype(F32).astype(BF16), preferred_element_type=F32).astype(BF16)
+    return lax.dot_general(
+        w_block, chosen.astype(F32).astype(BF16), (((0,), (0,)), ((), ())), preferred_element_type=F32
+    ).astype(BF16)
 
 
 def kernel(
     features_hbm, mask_hbm, update_hbm, atom_hbm, pair_hbm, bias_hbm, block_hbm, trial_hbm,
-    out_ref,
+    out_hbm,
     features_in, mask_in, w_update, w_atom, w_pair, bias, w_block, trial,
-    patches, mask_wide, x_hi, x_lo, y_hi, z_hi, y, z, placed, gather, select,
-    self_part, pair_part, masks, blocks, h_full, h_hi, h_lo,
-    load_sem, send_f, recv_f, send_x, recv_x,
+    patches, x_hi, x_lo, y_hi, z_hi, y, z, placed, gather, select,
+    self_part, pair_part, masks, blocks, h_full, h_hi, h_lo, result,
+    load_sem, out_sem, send_f, recv_f, send_x, recv_x,
 ):
     px, py = lax.axis_index("px"), lax.axis_index("py")
     nx, ny = lax.axis_size("px"), lax.axis_size("py")
@@ -63,13 +69,20 @@
     def device(side):
         return (lax.rem(px + side[0] + nx, nx), lax.rem(py + side[1] + ny, ny))
 
+    inner = lax.rem(py, LAYERS) != LAYERS - 1
+
+    def greet(sides):
+        for side in sides:
+            pl.semaphore_signal(barrier, inc=1, device_id=device(side), device_id_type=MESH)
+
     barrier = pltpu.get_barrier_semaphore()
-    for side in SIDES:
-        pl.semaphore_signal(barrier, inc=1, device_id=device(side), device_id_type=MESH)
+    greet(BACKWARD)
+    pl.when(inner)(lambda: greet(ACROSS))
 
     loads = []
     pairs = (
-        (trial_hbm, trial), (features_hbm, features_in), (mask_hbm, mask_in), (update_hbm, w_update),
+        (trial_hbm.at[:, :, :128], trial.at[0]), (trial_hbm.at[:, :, 128:], trial.at[1]),
+        (features_hbm, features_in), (mask_hbm, mask_in), (update_hbm, w_update),
         (atom_hbm, w_atom), (pair_hbm, w_pair), (bias_hbm, bias), (block_hbm, w_block),
     )
     for i, (source, target) in enumerate(pairs):
@@ -80,44 +93,55 @@
     for rows, columns in ((0, slice(11, 14)), (slice(1, 3), 13), (9, slice(0, 3)), (slice(7, 9), 0)):
         x_hi[rows, columns] = jnp.zeros_like(x_hi[rows, columns])
     x_lo[...] = jnp.zeros_like(x_lo)
-    mask_wide[...] = jnp.zeros_like(mask_wide)
-    trial_pad = jnp.zeros((8, PAD - ORBITALS, 256), F32)
-    for i in range(1, 3):
-        loads[i].wait()
+    loads[2].wait()
     patches[4, :, :128] = features_in[...].astype(F32).reshape(32, 128).astype(BF16)
-    mask_wide[:, :3] = mask_in[...].astype(F32).reshape(32, 3)
-    patches[4, :, 128:] = mask_wide[...].astype(BF16)
+    loads[3].wait()
+    row_of, column_of = iota((32, 8), 0), iota((32, 8), 1)
+    spread = (column_of == (row_of & 7)).astype(F32)
+    expand = (iota((32, 4), 1) == (iota((32, 4), 0) >> 3)).astype(BF16)
+    wide = jnp.zeros((32, 128), F32)
+    for k in range(3):
+        by_row = jnp.dot(expand, mask_in[k].astype(F32).astype(BF16), preferred_element_type=F32)
+        wide = wide + jnp.where(iota((32, 128), 1) == k, jnp.sum(by_row * spread, axis=1, keepdims=True), 0.0)
+    patches[4, :, 128:] = wide.astype(BF16)
     loads[0].wait()
+    loads[1].wait()
+    trial_pad = jnp.zeros((PAD - ORBITALS, 256), F32)
     for r in range(4):
-        wide = jnp.concatenate([trial[r], trial_pad], axis=1)
-        high = wide.astype(BF16)
-        x_hi[3 + r, 3:11] = high
-        x_lo[3 + r, 3:11] = (wide - high.astype(F32)).astype(BF16)
-
-    pl.semaphore_wait(barrier, len(SIDES))
-
-    feature_copies, vector_copies = [], []
+        for c in range(8):
+            atom = jnp.concatenate([trial[h, r, pl.ds(c, ORBITALS, stride=8), :] for h in range(2)], axis=1)
+            atom = jnp.concatenate([atom, trial_pad], axis=0)
+            high = atom.astype(BF16)
+            x_hi[3 + r, 3 + c] = high
+            x_lo[3 + r, 3 + c] = (atom - high.astype(F32)).astype(BF16)
+
+    feature_copies, vector_copies = {}, {}
     for i, side in enumerate(SIDES):
         mine = (1 - side[0]) * 3 + (1 - side[1])
-        copy = pltpu.make_async_remote_copy(
+        feature_copies[side] = pltpu.make_async_remote_copy(
             src_ref=patches.at[4], dst_ref=patches.at[mine], send_sem=send_f.at[i], recv_sem=recv_f.at[i],
             device_id=device(side), device_id_type=MESH,
         )
-        copy.start()
-        feature_copies.append(copy)
-    for i, side in enumerate(SIDES):
         width = 2 if side[0] * side[1] < 0 else 3
         from_r, to_r = span(side[0], 4, width)
         from_c, to_c = span(side[1], 8, width)
         shift = lambda s: slice(3 + s.start, 3 + s.stop)
-        copy = pltpu.make_async_remote_copy(
+        vector_copies[side] = pltpu.make_async_remote_copy(
             src_ref=x_hi.at[shift(from_r), shift(from_c)], dst_ref=x_hi.at[to_r, to_c],
             send_sem=send_x.at[i], recv_sem=recv_x.at[i], device_id=device(side), device_id_type=MESH,
         )
-        copy.start()
-        vector_copies.append(copy)
-
-    for i in range(3, 8):
+
+    def send(sides):
+        for side in sides:
+            feature_copies[side].start()
+        for side in sides:
+            vector_copies[side].start()
+
+    pl.semaphore_wait(barrier, jnp.where(inner, len(FORWARD) + len(ACROSS), len(FORWARD)))
+    send(FORWARD)
+    pl.when(inner)(lambda: send(ACROSS))
+
+    for i in range(4, 9):
         loads[i].wait()
     for i, (_, _, base, slot, transposed) in enumerate(BLOCKS):
         placed[i] = place_weights(w_block[...], base, transposed)
@@ -138,8 +162,12 @@
     select[...] = same.astype(F32).astype(BF16)
     gather[...] = near.astype(F32).astype(BF16)
 
-    for copy in feature_copies:
-        copy.wait_recv()
+    for side in FORWARD:
+        feature_copies[side].wait_recv()
+    send(BACKWARD)
+    pl.when(jnp.logical_not(inner))(lambda: send(ACROSS))
+    for side in BACKWARD + ACROSS:
+        feature_copies[side].wait_recv()
 
     around = patches[...].reshape(288, 256)
     picked = jnp.dot(select[...], around, preferred_element_type=F32)
@@ -194,8 +222,8 @@
 
     lax.fori_loop(0, 8, halves, 0)
 
-    for copy in vector_copies:
-        copy.wait_recv()
+    for side in SIDES:
+        vector_copies[side].wait_recv()
 
     def apply(vectors, r, g, first, last):
         c = 1 + 4 * g
@@ -241,24 +269,44 @@
             c, n = 1 + 4 * g + first, last - first
             value = (apply(z_hi, r, g, first, last) - CENTRE * z[r + 1, c : c + n]) * (2.0 / HALF_WIDTH)
             value = value - y[r + 1, c : c + n]
-            out_ref[r - 2, c - 3 : c - 3 + n] = value[:, :ORBITALS]
-        return carry
+            for h in range(2):
+                for k in range(n):
+                    result[h, r - 2, pl.ds(c - 3 + k, ORBITALS, stride=8), :] = value[
+                        k, :ORBITALS, 128 * h : 128 * h + 128
+                    ]
+        for h in range(2):
+            out_copy(r - 2, h).start()
+        return carry
+
+    def out_copy(r, h):
+        return pltpu.make_async_copy(
+            result.at[h, r], out_hbm.at[r, :, 128 * h : 128 * h + 128], out_sem.at[h, r]
+        )
 
     lax.fori_loop(2, 6, third_step, 0)
 
-    for copy in feature_copies + vector_copies:
-        copy.wait_send()
+    for side in SIDES:
+        feature_copies[side].wait_send()
+        vector_copies[side].wait_send()
+    for r in range(4):
+        for h in range(2):
+            out_copy(r, h).wait()
 
 
 def per_device(features, pair_mask, w_update, w_atom, w_pair, slot_bias, w_block, trial):
+    pair_mask = pair_mask.transpose(2, 0, 1)
+    w_block = w_block.T
+    rows, columns, _, width = trial.shape
+    trial = trial.transpose(0, 2, 1, 3).reshape(rows, ORBITALS * columns, width)
+    halves = (2, rows, ORBITALS * columns, 128)
     vectors = (10, 14, PAD, 256)
     sides = pltpu.SemaphoreType.DMA((len(SIDES),))
-    return pl.pallas_call(
+    filtered = pl.pallas_call(
         kernel,
         name="filter",
         out_shape=jax.ShapeDtypeStruct(trial.shape, trial.dtype),
         in_specs=[pl.BlockSpec(memory_space=pl.ANY)] * 8,
-        out_specs=pl.BlockSpec(memory_space=pltpu.VMEM),
+        out_specs=pl.BlockSpec(memory_space=pl.ANY),
         scratch_shapes=[
             pltpu.VMEM(features.shape, BF16),
             pltpu.VMEM(pair_mask.shape, jnp.int32),
@@ -267,9 +315,8 @@
             pltpu.VMEM(w_pair.shape, BF16),
             pltpu.VMEM(slot_bias.shape, F32),
             pltpu.VMEM(w_block.shape, BF16),
-            pltpu.VMEM(trial.shape, F32),
+            pltpu.VMEM(halves, F32),
             pltpu.VMEM((9, 32, 256), BF16),
-            pltpu.VMEM((32, 128), F32),
             pltpu.VMEM(vectors, BF16),
             pltpu.VMEM(vectors, BF16),
             pltpu.VMEM(vectors, BF16),
@@ -286,16 +333,19 @@
             pltpu.VMEM((2, 1536, 128), F32),
             pltpu.VMEM((1536, 256), BF16),
             pltpu.VMEM((1536, 256), BF16),
-            pltpu.SemaphoreType.DMA((8,)),
+            pltpu.VMEM(halves, F32),
+            pltpu.SemaphoreType.DMA((9,)),
+            pltpu.SemaphoreType.DMA((2, 4)),
             sides,
             sides,
             sides,
             sides,
         ],
         compiler_params=pltpu.CompilerParams(
-            collective_id=0, has_side_effects=True, vmem_limit_bytes=48 * 2**20
+            collective_id=0, has_side_effects=True, vmem_limit_bytes=60 * 2**20
         ),
     )(features, pair_mask, w_update, w_atom, w_pair, slot_bias, w_block, trial)
+    return filtered.reshape(rows, ORBITALS, columns, width).transpose(0, 2, 1, 3)
 
 
 def solution(mesh):

time: 42.4 us -> 35.5 us (0.84)
  Pallas kernels: 38.2 us -> 33.5 us
  local copies, waits for them, and re-layouts: 3.88 us -> 1.79 us
    pallas_call x1, Pallas kernels: 38.2 us -> 33.5 us  [per_device(): pl.pallas_call(kernel, name='filter', out_shape=jax.ShapeDtypeStruct(tria...]
    unnamed x13 -> x1, local copies, waits for them, and re-layouts: 2.87 us -> 1.79 us
    pallas_call x1 -> x0, local copies, waits for them, and re-layouts: 1.01 us -> none  [per_device(): pl.pallas_call(kernel, name='filter', out_shape=jax.ShapeDtypeStruct(tria...]
where the time goes in v2:
time: 35.5 us; the launch traced here: 35.3 us
  Pallas kernels  33.5 us (94%)
  local copies, waits for them, and re-layouts  1.79 us (5%)
    pallas_call x1, Pallas kernels, per_device(): pl.pallas_call(kernel, name='filter', out_shape=jax.ShapeDtypeStruct(tria...  33.5 us
    unnamed x1, local copies, waits for them, and re-layouts  1.79 us

profile of v2, /device:TPU:8, one launch (start us, length us, event | category | flops | bytes accessed | tf_op | source)
XLA Modules:
  0.0 35.3 jit_solution(14715096477114379460)
XLA Ops:
  0.0 33.5 %filter.1 = f32[4,104,256]{2,1,0:T(8,128)} custom-call(bf16[4,8,128]{2,1,0:T(8,128)(2,1)} %features_hbm.1, s32[3,4,8]{2,1,0:T(4,128)} %bitcast.11, bf16[128,128]{1,0:T(8,128)(2,1)} %update_hbm.1, bf16[128,128]{1,0:T(8,128)(2,1)} %atom_hbm.1, bf16[128,128]{1,0:T(8,128)(2,1)} %pair_hbm.1, f32[4,128]{1,0:T(4,128)} %bias_hbm.1, bf16[169,128]{1,0:T(8,128)(2,1)} %bitcast.10, ...), custom_call_target="tpu_custom_call" | custom-call | tf_op jit(solution)/shard_map/filter/pallas_call | solution.py:304
  33.5 1.8 %copy.10 = f32[4,8,13,256]{3,1,2,0:T(8,128)} copy(f32[4,8,13,256]{3,1,2,0:T(8,128)} %bitcast.8) | data formatting | bytes 851968

commit v3 on v2

v3 whole, which is shorter than its diff:
```python
import functools

import jax
import jax.numpy as jnp
from jax import lax
from jax.experimental import pallas as pl
from jax.experimental.pallas import tpu as pltpu
from jax.sharding import PartitionSpec as P

ORBITALS = 13
PAD = 16
CENTRE = 4.0
HALF_WIDTH = 24.0
MESH = pl.DeviceIdType.MESH
F32 = jnp.float32
BF16 = jnp.bfloat16

FORWARD = ((0, 1), (1, 1), (-1, 1))
BACKWARD = ((0, -1), (-1, -1), (1, -1))
ACROSS = ((1, 0), (-1, 0))
SIDES = FORWARD + BACKWARD + ACROSS
LAYERS = 12
UNROLL = True
BLOCKS = (
    (-1, -1, 0, 2, True),
    (-1, 0, 1, 1, True),
    (0, -1, 5, 0, True),
    (0, 0, 6, 3, False),
    (0, 1, 7, 0, False),
    (1, 0, 11, 1, False),
    (1, 1, 12, 2, False),
)


def span(step, size, width):
    if step > 0:
        return slice(size - width, size), slice(3 - width, 3)
    if step < 0:
        return slice(0, width), slice(3 + size, 3 + size + width)
    return slice(0, size), slice(3, 3 + size)


def iota(shape, axis):
    return lax.broadcasted_iota(jnp.int32, shape, axis)


def place_weights(w_block, base, transposed):
    lane = iota((ORBITALS * ORBITALS, 256), 1)
    source = iota((ORBITALS * ORBITALS, 256), 0)
    b = lane & 15
    a = 8 * (lane >> 7) + ((base - ((lane >> 4) & 7)) & 7)
    entry = b * ORBITALS + a if transposed else a * ORBITALS + b
    chosen = (source == entry) & (a < ORBITALS) & (b < ORBITALS)
    return lax.dot_general(
        w_block, chosen.astype(F32).astype(BF16), (((0,), (0,)), ((), ())), preferred_element_type=F32
    ).astype(BF16)


def kernel(
    features_hbm, mask_hbm, update_hbm, atom_hbm, pair_hbm, bias_hbm, block_hbm, trial_hbm,
    out_ref,
    features_in, mask_in, w_update, w_atom, w_pair, bias, w_block, trial,
    patches, x_hi, x_lo, y_hi, z_hi, y, z, placed, gather, select,
    self_part, pair_part, masks, blocks, h_full, h,
    load_sem, send_f, recv_f, send_x, recv_x,
):
    px, py = lax.axis_index("px"), lax.axis_index("py")
    nx, ny = lax.axis_size("px"), lax.axis_size("py")

    def device(side):
        return (lax.rem(px + side[0] + nx, nx), lax.rem(py + side[1] + ny, ny))

    layer = lax.rem(py, LAYERS)
    first, last = layer == 0, layer == LAYERS - 1

    def greet(sides):
        for side in sides:
            pl.semaphore_signal(barrier, inc=1, device_id=device(side), device_id_type=MESH)

    barrier = pltpu.get_barrier_semaphore()
    greet(BACKWARD)
    pl.when(jnp.logical_not(last))(lambda: greet(ACROSS))
    pl.when(layer < LAYERS - 2)(lambda: greet(FORWARD))

    loads = []
    pairs = (
        (trial_hbm.at[:, :, :128], trial.at[0]), (trial_hbm.at[:, :, 128:], trial.at[1]),
        (features_hbm, features_in), (mask_hbm, mask_in), (update_hbm, w_update),
        (atom_hbm, w_atom), (pair_hbm, w_pair), (bias_hbm, bias), (block_hbm, w_block),
    )
    for i, (source, target) in enumerate(pairs):
        copy = pltpu.make_async_copy(source, target, load_sem.at[i])
        copy.start()
        loads.append(copy)

    for rows, columns in ((0, slice(11, 14)), (slice(1, 3), 13), (9, slice(0, 3)), (slice(7, 9), 0)):
        x_hi[rows, columns] = jnp.zeros_like(x_hi[rows, columns])
    x_lo[...] = jnp.zeros_like(x_lo)
    loads[2].wait()
    patches[4, :, :128] = features_in[...].astype(F32).reshape(32, 128).astype(BF16)
    loads[3].wait()
    row_of, column_of = iota((32, 8), 0), iota((32, 8), 1)
    spread = (column_of == (row_of & 7)).astype(F32)
    expand = (iota((32, 4), 1) == (iota((32, 4), 0) >> 3)).astype(BF16)
    wide = jnp.zeros((32, 128), F32)
    for k in range(3):
        by_row = jnp.dot(expand, mask_in[k].astype(F32).astype(BF16), preferred_element_type=F32)
        wide = wide + jnp.where(iota((32, 128), 1) == k, jnp.sum(by_row * spread, axis=1, keepdims=True), 0.0)
    patches[4, :, 128:] = wide.astype(BF16)
    loads[0].wait()
    loads[1].wait()
    trial_pad = jnp.zeros((PAD - ORBITALS, 256), F32)
    for r in range(4):
        for c in range(8):
            atom = jnp.concatenate([trial[h, r, pl.ds(c, ORBITALS, stride=8), :] for h in range(2)], axis=1)
            atom = jnp.concatenate([atom, trial_pad], axis=0)
            high = atom.astype(BF16)
            x_hi[3 + r, 3 + c] = high
            x_lo[3 + r, 3 + c] = (atom - high.astype(F32)).astype(BF16)

    feature_copies, vector_copies = {}, {}
    for i, side in enumerate(SIDES):
        mine = (1 - side[1]) * 3 + (1 - side[0])
        feature_copies[side] = pltpu.make_async_remote_copy(
            src_ref=patches.at[4], dst_ref=patches.at[mine], send_sem=send_f.at[i], recv_sem=recv_f.at[i],
            device_id=device(side), device_id_type=MESH,
        )
        width = 2 if side[0] * side[1] < 0 else 3
        from_r, to_r = span(side[0], 4, width)
        from_c, to_c = span(side[1], 8, width)
        shift = lambda s: slice(3 + s.start, 3 + s.stop)
        vector_copies[side] = pltpu.make_async_remote_copy(
            src_ref=x_hi.at[shift(from_r), shift(from_c)], dst_ref=x_hi.at[to_r, to_c],
            send_sem=send_x.at[i], recv_sem=recv_x.at[i], device_id=device(side), device_id_type=MESH,
        )

    def send(sides):
        for side in sides:
            feature_copies[side].start()
        for side in sides:
            vector_copies[side].start()

    pl.semaphore_wait(barrier, jnp.where(last, 3, jnp.where(first, 5, 8)))
    send(FORWARD)
    pl.when(jnp.logical_not(last))(lambda: send(ACROSS))
    pl.when(jnp.logical_not(first | last))(lambda: send(BACKWARD))

    for i in range(4, 9):
        loads[i].wait()
    for i, (_, _, base, slot, transposed) in enumerate(BLOCKS):
        placed[i] = place_weights(w_block[...], base, transposed)
    placed[7] = place_weights(w_block[...], BLOCKS[3][2], True)
    y_hi[...] = jnp.zeros_like(y_hi)
    z_hi[...] = jnp.zeros_like(z_hi)
    h_full[...] = jnp.zeros_like(h_full)

    point = iota((160, 1), 0)
    cell = iota((1, 192), 1)
    patch = cell >> 5
    patch_column = (patch >= 3).astype(jnp.int32)
    cell_row = (patch - 3 * patch_column) * 4 - 4 + ((cell >> 3) & 3)
    for i, (first_patch, first_point) in enumerate(((0, 1), (-8, -3))):
        down = cell_row - ((point & 15) - 3)
        right = (patch_column * 8 + first_patch + (cell & 7)) - ((point >> 4) + first_point)
        same = (down == 0) & (right == 0)
        near = (jnp.abs(down) <= 1) & (jnp.abs(right) <= 1) & (down + right != 0) | (
            (down == right) & (jnp.abs(down) == 1)
        )
        select[i] = same.astype(F32).astype(BF16)
        gather[i] = near.astype(F32).astype(BF16)

    lane_slot = iota((8, 128), 1) >> 4

    def build(left):
        i, columns = (1, 6) if left else (0, 10)
        atoms, wide = columns * 16, columns - 2
        around = (patches[:6] if left else patches[3:]).reshape(192, 256)
        picked = jnp.dot(select[i, :atoms], around, preferred_element_type=F32)
        gathered = jnp.dot(gather[i, :atoms], around[:, :128], preferred_element_type=F32)
        own = picked[:, :128]
        update = jax.nn.silu(jnp.dot(gathered.astype(BF16), w_update[...], preferred_element_type=F32))
        refined = (own + update).astype(BF16)
        shape = (columns, 16, 128)
        self_part[:columns] = jnp.dot(refined, w_atom[...], preferred_element_type=F32).reshape(shape)
        pair_part[:columns] = jnp.dot(own.astype(BF16), w_pair[...], preferred_element_type=F32).reshape(shape)
        masks[:columns] = picked[:, 128:].reshape(shape)

        for i, (dr, dc, _, slot, transposed) in enumerate(BLOCKS):
            r0, c0 = (1 + dr, 1 + dc) if transposed else (1, 1)
            r1, c1 = (1, 1) if transposed else (1 + dr, 1 + dc)
            message = jax.nn.silu(
                self_part[c0 : c0 + wide, r0 : r0 + 8]
                + pair_part[c1 : c1 + wide, r1 : r1 + 8]
                + bias[slot : slot + 1]
            )
            if slot < 3:
                message = message * masks[c0 : c0 + wide, r0 : r0 + 8, slot : slot + 1]
            message = message.astype(BF16).reshape(wide * 8, 128)
            block = jnp.dot(message, placed[i], preferred_element_type=F32)
            if slot == 3:
                block = 0.5 * (block + jnp.dot(message, placed[7], preferred_element_type=F32))
            blocks[i, :wide] = block.reshape(wide, 8, 256)

        for g in (0,) if left else (1, 2):
            for c in range(4):
                at = c + 4 * max(g - 1, 0)
                for a in range(ORBITALS):
                    half = slice(128 * (a // 8), 128 * (a // 8) + 128)
                    for part in range(2):
                        value = jnp.zeros((8, 128), F32)
                        for i, (_, _, base, _, _) in enumerate(BLOCKS):
                            if (base + c) // 8 == part:
                                value = jnp.where(lane_slot == (base - a) % 8, blocks[i, at, :, half], value)
                        turn = (c + a) * 16 % 128
                        if turn:
                            value = pltpu.roll(value, turn, axis=1)
                        h_full[g, part, pl.ds(c * 16 + a, 8, stride=64), :] = value

            def halves(r, carry):
                rows = pl.ds(pl.multiple_of(r * 64, 64), 64)
                full = jnp.concatenate([h_full[g, 0, rows, :], h_full[g, 1, rows, :]], axis=1)
                high = full.astype(BF16)
                h[g, r, :64] = high
                h[g, r, 64:] = (full - high.astype(F32)).astype(BF16)
                return carry

            lax.fori_loop(0, 8, halves, 0, unroll=UNROLL)

    def apply(vectors, r, g, begin=0, end=4):
        c = 1 + 4 * g
        weights = jnp.concatenate(
            [
                vectors[r, c - 1 : c + 4].reshape(80, 256),
                vectors[r + 1, c - 1 : c + 5].reshape(96, 256),
                vectors[r + 2, c : c + 5].reshape(80, 256),
            ],
            axis=0,
        )
        rows = slice(16 * begin, 16 * end)
        parts = jnp.concatenate([h[g, r, :64][rows], h[g, r, 64:][rows]], axis=0)
        total = jnp.dot(parts, weights, preferred_element_type=F32)
        size = 16 * (end - begin)
        return (total[:size] + total[size:]).reshape(end - begin, PAD, 256)

    def start(r, c, n):
        return x_hi[r, c : c + n].astype(F32) + x_lo[r, c : c + n].astype(F32)

    def first_step(groups):
        def row(r, carry):
            for g in groups:
                c = 1 + 4 * g
                value = (apply(x_hi, r, g) - CENTRE * start(r + 1, c, 4)) * (1.0 / HALF_WIDTH)
                y[r + 1, c : c + 4] = value
                y_hi[r + 1, c : c + 4] = value.astype(BF16)
            return carry

        lax.fori_loop(0, 8, row, 0, unroll=UNROLL)

    def second_step(groups):
        def row(r, carry):
            for g in groups:
                c = 1 + 4 * g
                value = (apply(y_hi, r, g) - CENTRE * y[r + 1, c : c + 4]) * (2.0 / HALF_WIDTH)
                value = value - start(r + 1, c, 4)
                z[r + 1, c : c + 4] = value
                z_hi[r + 1, c : c + 4] = value.astype(BF16)
            return carry

        lax.fori_loop(1, 7, row, 0, unroll=UNROLL)

    def third_row(r, carry):
        for g, begin, end in ((0, 2, 4), (1, 0, 4), (2, 0, 2)):
            c, n = 1 + 4 * g + begin, end - begin
            value = (apply(z_hi, r, g, begin, end) - CENTRE * z[r + 1, c : c + n]) * (2.0 / HALF_WIDTH)
            value = value - y[r + 1, c : c + n]
            for half in range(2):
                for k in range(n):
                    out_ref[pl.ds((r - 2) * 208 + half * 8 + c - 3 + k, ORBITALS, stride=16), :] = value[
                        k, :ORBITALS, 128 * half : 128 * half + 128
                    ]
        return carry

    def late():
        feature_copies[FORWARD[0]].wait_recv()
        pl.when(last)(lambda: send(ACROSS))
        for side in FORWARD[1:]:
            feature_copies[side].wait_recv()
        pl.when(first | last)(lambda: send(BACKWARD))

    pl.when(last)(late)
    for side in BACKWARD + ACROSS:
        feature_copies[side].wait_recv()
    build(left=False)
    for side in BACKWARD + ACROSS:
        vector_copies[side].wait_recv()
    first_step((1, 2))
    second_step((2,))

    pl.when(jnp.logical_not(last))(late)
    build(left=True)
    for side in FORWARD:
        vector_copies[side].wait_recv()
    first_step((0,))
    second_step((0, 1))
    lax.fori_loop(2, 6, third_row, 0, unroll=UNROLL)

    for side in SIDES:
        feature_copies[side].wait_send()
        vector_copies[side].wait_send()


def per_device(features, pair_mask, w_update, w_atom, w_pair, slot_bias, w_block, trial):
    pair_mask = pair_mask.transpose(2, 0, 1)
    w_block = w_block.T
    rows, columns, _, width = trial.shape
    trial = trial.transpose(0, 2, 1, 3).reshape(rows, ORBITALS * columns, width)
    halves = (2, rows, ORBITALS * columns, 128)
    vectors = (10, 14, PAD, 256)
    sides = pltpu.SemaphoreType.DMA((len(SIDES),))
    filtered = pl.pallas_call(
        kernel,
        name="filter",
        out_shape=jax.ShapeDtypeStruct((rows * ORBITALS * 2 * columns, 128), F32),
        in_specs=[pl.BlockSpec(memory_space=pltpu.HBM)] * 8,
        out_specs=pl.BlockSpec(memory_space=pltpu.VMEM),
        scratch_shapes=[
            pltpu.VMEM(features.shape, BF16),
            pltpu.VMEM(pair_mask.shape, jnp.int32),
            pltpu.VMEM(w_update.shape, BF16),
            pltpu.VMEM(w_atom.shape, BF16),
            pltpu.VMEM(w_pair.shape, BF16),
            pltpu.VMEM(slot_bias.shape, F32),
            pltpu.VMEM(w_block.shape, BF16),
            pltpu.VMEM(halves, F32),
            pltpu.VMEM((9, 32, 256), BF16),
            pltpu.VMEM(vectors, BF16),
            pltpu.VMEM(vectors, BF16),
            pltpu.VMEM(vectors, BF16),
            pltpu.VMEM(vectors, BF16),
            pltpu.VMEM(vectors, F32),
            pltpu.VMEM(vectors, F32),
            pltpu.VMEM((8, 128, 256), BF16),
            pltpu.VMEM((2, 160, 192), BF16),
            pltpu.VMEM((2, 160, 192), BF16),
            pltpu.VMEM((10, 16, 128), F32),
            pltpu.VMEM((10, 16, 128), F32),
            pltpu.VMEM((10, 16, 128), F32),
            pltpu.VMEM((7, 8, 8, 256), F32),
            pltpu.VMEM((3, 2, 512, 128), F32),
            pltpu.VMEM((3, 8, 128, 256), BF16),
            pltpu.SemaphoreType.DMA((9,)),
            sides,
            sides,
            sides,
            sides,
        ],
        compiler_params=pltpu.CompilerParams(
            collective_id=0, has_side_effects=True, vmem_limit_bytes=40 * 2**20
        ),
    )(
        *(
            pltpu.with_memory_space_constraint(array, pltpu.HBM)
            for array in (features, pair_mask, w_update, w_atom, w_pair, slot_bias, w_block, trial)
        )
    )
    filtered = filtered.reshape(rows, ORBITALS, 2, columns, 128).transpose(0, 1, 3, 2, 4)
    return filtered.reshape(rows, ORBITALS, columns, width).transpose(0, 2, 1, 3)


def solution(mesh):
    return jax.shard_map(
        per_device,
        mesh=mesh,
        in_specs=(
            P("px", "py", None),
            P("px", "py", None),
            P(),
            P(),
            P(),
            P(),
            P(),
            P("px", "py", None, None),
        ),
        out_specs=P("px", "py", None, None),
        check_vma=False,
    )
```

time: 35.5 us -> 29.5 us (0.83)
  the two profiles are of different devices: /device:TPU:8 before, /device:TPU:63 now
where the time goes in v3:
time: 29.5 us; the launch traced here: 29.4 us
  Pallas kernels  28.6 us (97%)
  local copies, waits for them, and re-layouts  0.76 us (3%)
    pallas_call x1, Pallas kernels, per_device(): pl.pallas_call(kernel, name='filter', out_shape=jax.ShapeDtypeStruct((row...  28.6 us
    unnamed x1, local copies, waits for them, and re-layouts  0.76 us

profile of v3, /device:TPU:63, one launch (start us, length us, event | category | flops | bytes accessed | tf_op | source)
XLA Modules:
  0.0 29.4 jit_solution(14029975993430656457)
XLA Ops:
  0.0 28.6 %filter.1 = f32[832,128]{1,0:T(8,128)S(1)} custom-call(bf16[4,8,128]{2,1,0:T(8,128)(2,1)} %features_hbm.1, s32[3,4,8]{2,1,0:T(4,128)} %bitcast.15, bf16[128,128]{1,0:T(8,128)(2,1)} %update_hbm.1, bf16[128,128]{1,0:T(8,128)(2,1)} %atom_hbm.1, bf16[128,128]{1,0:T(8,128)(2,1)} %pair_hbm.1, f32[4,128]{1,0:T(4,128)} %bias_hbm.1, bf16[169,128]{1,0:T(8,128)(2,1)} %bitcast.14, ...), custom_call_target="tpu_custom_call" | custom-call | tf_op jit(solution)/shard_map/filter/pallas_call | solution.py:320
  28.6 0.8 %copy.10 = f32[4,8,13,256]{3,1,2,0:T(8,128)} copy(f32[4,8,13,256]{3,1,2,0:T(8,128)S(1)} %bitcast.12) | data formatting | bytes 851968

commit v4 on v3

--- a/solution.py
+++ b/solution.py
@@ -15,8 +15,8 @@
 F32 = jnp.float32
 BF16 = jnp.bfloat16
 
-FORWARD = ((0, 1), (1, 1), (-1, 1))
-BACKWARD = ((0, -1), (-1, -1), (1, -1))
+FORWARD = ((1, 1), (-1, 1), (0, 1))
+BACKWARD = ((-1, -1), (1, -1), (0, -1))
 ACROSS = ((1, 0), (-1, 0))
 SIDES = FORWARD + BACKWARD + ACROSS
 LAYERS = 12
@@ -62,7 +62,7 @@
     features_in, mask_in, w_update, w_atom, w_pair, bias, w_block, trial,
     patches, x_hi, x_lo, y_hi, z_hi, y, z, placed, gather, select,
     self_part, pair_part, masks, blocks, h_full, h,
-    load_sem, send_f, recv_f, send_x, recv_x,
+    load_sem, answered, send_f, recv_f, send_x, recv_x,
 ):
     px, py = lax.axis_index("px"), lax.axis_index("py")
     nx, ny = lax.axis_size("px"), lax.axis_size("py")
@@ -78,7 +78,7 @@
             pl.semaphore_signal(barrier, inc=1, device_id=device(side), device_id_type=MESH)
 
     barrier = pltpu.get_barrier_semaphore()
-    greet(BACKWARD)
+    pl.when(layer != 1)(lambda: greet(BACKWARD))
     pl.when(jnp.logical_not(last))(lambda: greet(ACROSS))
     pl.when(layer < LAYERS - 2)(lambda: greet(FORWARD))
 
@@ -92,31 +92,6 @@
         copy = pltpu.make_async_copy(source, target, load_sem.at[i])
         copy.start()
         loads.append(copy)
-
-    for rows, columns in ((0, slice(11, 14)), (slice(1, 3), 13), (9, slice(0, 3)), (slice(7, 9), 0)):
-        x_hi[rows, columns] = jnp.zeros_like(x_hi[rows, columns])
-    x_lo[...] = jnp.zeros_like(x_lo)
-    loads[2].wait()
-    patches[4, :, :128] = features_in[...].astype(F32).reshape(32, 128).astype(BF16)
-    loads[3].wait()
-    row_of, column_of = iota((32, 8), 0), iota((32, 8), 1)
-    spread = (column_of == (row_of & 7)).astype(F32)
-    expand = (iota((32, 4), 1) == (iota((32, 4), 0) >> 3)).astype(BF16)
-    wide = jnp.zeros((32, 128), F32)
-    for k in range(3):
-        by_row = jnp.dot(expand, mask_in[k].astype(F32).astype(BF16), preferred_element_type=F32)
-        wide = wide + jnp.where(iota((32, 128), 1) == k, jnp.sum(by_row * spread, axis=1, keepdims=True), 0.0)
-    patches[4, :, 128:] = wide.astype(BF16)
-    loads[0].wait()
-    loads[1].wait()
-    trial_pad = jnp.zeros((PAD - ORBITALS, 256), F32)
-    for r in range(4):
-        for c in range(8):
-            atom = jnp.concatenate([trial[h, r, pl.ds(c, ORBITALS, stride=8), :] for h in range(2)], axis=1)
-            atom = jnp.concatenate([atom, trial_pad], axis=0)
-            high = atom.astype(BF16)
-            x_hi[3 + r, 3 + c] = high
-            x_lo[3 + r, 3 + c] = (atom - high.astype(F32)).astype(BF16)
 
     feature_copies, vector_copies = {}, {}
     for i, side in enumerate(SIDES):
@@ -134,16 +109,68 @@
             send_sem=send_x.at[i], recv_sem=recv_x.at[i], device_id=device(side), device_id_type=MESH,
         )
 
-    def send(sides):
+    def send_features(sides):
         for side in sides:
             feature_copies[side].start()
+
+    def send_vectors(sides):
         for side in sides:
             vector_copies[side].start()
 
-    pl.semaphore_wait(barrier, jnp.where(last, 3, jnp.where(first, 5, 8)))
-    send(FORWARD)
-    pl.when(jnp.logical_not(last))(lambda: send(ACROSS))
-    pl.when(jnp.logical_not(first | last))(lambda: send(BACKWARD))
+    def send(sides):
+        send_features(sides)
+        send_vectors(sides)
+
+    def answer():
+        pl.semaphore_wait(barrier, len(FORWARD))
+        for side in FORWARD:
+            pl.semaphore_signal(answered, inc=1, device_id=device(side), device_id_type=MESH)
+
+    pl.when(last)(answer)
+
+    loads[2].wait()
+    patches[4, :, :128] = features_in[...].astype(F32).reshape(32, 128).astype(BF16)
+    loads[3].wait()
+    diagonal = (iota((4, 8, 8), 1) == iota((4, 8, 8), 2)).astype(F32)
+    wide = jnp.zeros((4, 8, 128), F32)
+    for k in range(3):
+        by_row = jnp.broadcast_to(mask_in[k].astype(F32)[:, None, :], (4, 8, 8))
+        in_mask = jnp.sum(by_row * diagonal, axis=2, keepdims=True)
+        wide = wide + jnp.where(iota((4, 8, 128), 2) == k, in_mask, 0.0)
+    patches[4, :, 128:] = wide.reshape(32, 128).astype(BF16)
+    pl.when(last)(lambda: send_features(FORWARD))
+    loads[0].wait()
+    loads[1].wait()
+    trial_pad = jnp.zeros((PAD - ORBITALS, 256), F32)
+
+    def convert(columns):
+        for r in range(4):
+            for c in columns:
+                atom = jnp.concatenate(
+                    [trial[h, r, pl.ds(c, ORBITALS, stride=8), :] for h in range(2)], axis=1
+                )
+                atom = jnp.concatenate([atom, trial_pad], axis=0)
+                high = atom.astype(BF16)
+                x_hi[3 + r, 3 + c] = high
+                x_lo[3 + r, 3 + c] = (atom - high.astype(F32)).astype(BF16)
+
+    convert(range(5, 8))
+    pl.when(last)(lambda: send_vectors(FORWARD))
+    convert(range(5))
+
+    def send_all():
+        pl.semaphore_wait(barrier, jnp.where(first, 2, 8))
+        send(ACROSS)
+        pl.when(jnp.logical_not(first))(lambda: send(FORWARD + BACKWARD))
+
+    pl.when(jnp.logical_not(last))(send_all)
+
+    for rows, columns in ((0, slice(11, 14)), (slice(1, 3), 13), (9, slice(0, 3)), (slice(7, 9), 0)):
+        x_hi[rows, columns] = jnp.zeros_like(x_hi[rows, columns])
+    for rows, columns in (
+        (slice(0, 3), slice(0, 14)), (slice(7, 10), slice(0, 14)), (slice(3, 7), slice(0, 3)), (slice(3, 7), slice(11, 14))
+    ):
+        x_lo[rows, columns] = jnp.zeros_like(x_lo[rows, columns])
 
     for i in range(4, 9):
         loads[i].wait()
@@ -281,14 +308,22 @@
         return carry
 
     def late():
-        feature_copies[FORWARD[0]].wait_recv()
+        def send_back():
+            pl.semaphore_wait(answered, len(BACKWARD))
+            send(BACKWARD)
+
+        pl.when(first)(send_back)
+        feature_copies[FORWARD[2]].wait_recv()
         pl.when(last)(lambda: send(ACROSS))
-        for side in FORWARD[1:]:
+        for side in FORWARD[:2]:
             feature_copies[side].wait_recv()
-        pl.when(first | last)(lambda: send(BACKWARD))
+        pl.when(last)(lambda: send(BACKWARD))
 
     pl.when(last)(late)
-    for side in BACKWARD + ACROSS:
+    for side in BACKWARD:
+        feature_copies[side].wait_recv()
+    pl.when(first)(lambda: send(FORWARD))
+    for side in ACROSS:
         feature_copies[side].wait_recv()
     build(left=False)
     for side in BACKWARD + ACROSS:
@@ -349,6 +384,7 @@
             pltpu.VMEM((3, 2, 512, 128), F32),
             pltpu.VMEM((3, 8, 128, 256), BF16),
             pltpu.SemaphoreType.DMA((9,)),
+            pltpu.SemaphoreType.REGULAR,
             sides,
             sides,
             sides,

time: 29.5 us -> 28.2 us (0.956)
  the two profiles are of different devices: /device:TPU:63 before, /device:TPU:39 now
where the time goes in v4:
time: 28.2 us; the launch traced here: 28 us
  Pallas kernels  27.2 us (96%)
  local copies, waits for them, and re-layouts  0.76 us (3%)
    pallas_call x1, Pallas kernels, per_device(): pl.pallas_call(kernel, name='filter', out_shape=jax.ShapeDtypeStruct((row...  27.2 us
    unnamed x1, local copies, waits for them, and re-layouts  0.76 us

profile of v4, /device:TPU:39, one launch (start us, length us, event | category | flops | bytes accessed | tf_op | source)
XLA Modules:
  0.0 28.0 jit_solution(6417699455706343619)
XLA Ops:
  0.0 27.2 %filter.1 = f32[832,128]{1,0:T(8,128)S(1)} custom-call(bf16[4,8,128]{2,1,0:T(8,128)(2,1)} %features_hbm.1, s32[3,4,8]{2,1,0:T(4,128)} %bitcast.15, bf16[128,128]{1,0:T(8,128)(2,1)} %update_hbm.1, bf16[128,128]{1,0:T(8,128)(2,1)} %atom_hbm.1, bf16[128,128]{1,0:T(8,128)(2,1)} %pair_hbm.1, f32[4,128]{1,0:T(4,128)} %bias_hbm.1, bf16[169,128]{1,0:T(8,128)(2,1)} %bitcast.14, ...), custom_call_target="tpu_custom_call" | custom-call | tf_op jit(solution)/shard_map/filter/pallas_call | solution.py:355
  27.2 0.8 %copy.10 = f32[4,8,13,256]{3,1,2,0:T(8,128)} copy(f32[4,8,13,256]{3,1,2,0:T(8,128)S(1)} %bitcast.12) | data formatting | bytes 851968

commit v5 on v4

--- a/solution.py
+++ b/solution.py
@@ -96,8 +96,9 @@
     feature_copies, vector_copies = {}, {}
     for i, side in enumerate(SIDES):
         mine = (1 - side[1]) * 3 + (1 - side[0])
+        near_columns = slice(16, 32) if side in FORWARD else slice(0, 16) if side in BACKWARD else slice(0, 32)
         feature_copies[side] = pltpu.make_async_remote_copy(
-            src_ref=patches.at[4], dst_ref=patches.at[mine], send_sem=send_f.at[i], recv_sem=recv_f.at[i],
+            src_ref=patches.at[4, near_columns], dst_ref=patches.at[mine, near_columns], send_sem=send_f.at[i], recv_sem=recv_f.at[i],
             device_id=device(side), device_id_type=MESH,
         )
         width = 2 if side[0] * side[1] < 0 else 3
@@ -129,7 +130,7 @@
     pl.when(last)(answer)
 
     loads[2].wait()
-    patches[4, :, :128] = features_in[...].astype(F32).reshape(32, 128).astype(BF16)
+    atoms = features_in[...].astype(F32).reshape(32, 128)
     loads[3].wait()
     diagonal = (iota((4, 8, 8), 1) == iota((4, 8, 8), 2)).astype(F32)
     wide = jnp.zeros((4, 8, 128), F32)
@@ -137,7 +138,9 @@
         by_row = jnp.broadcast_to(mask_in[k].astype(F32)[:, None, :], (4, 8, 8))
         in_mask = jnp.sum(by_row * diagonal, axis=2, keepdims=True)
         wide = wide + jnp.where(iota((4, 8, 128), 2) == k, in_mask, 0.0)
-    patches[4, :, 128:] = wide.reshape(32, 128).astype(BF16)
+    atoms = jnp.concatenate([atoms, wide.reshape(32, 128)], axis=1).astype(BF16)
+    by_column = (iota((32, 32), 0) >> 2) + 8 * (iota((32, 32), 0) & 3) == iota((32, 32), 1)
+    patches[4] = jnp.dot(by_column.astype(F32).astype(BF16), atoms, preferred_element_type=F32).astype(BF16)
     pl.when(last)(lambda: send_features(FORWARD))
     loads[0].wait()
     loads[1].wait()
@@ -165,6 +168,8 @@
 
     pl.when(jnp.logical_not(last))(send_all)
 
+    patches[:3, :16] = jnp.zeros((3, 16, 256), BF16)
+    patches[6:, 16:] = jnp.zeros((3, 16, 256), BF16)
     for rows, columns in ((0, slice(11, 14)), (slice(1, 3), 13), (9, slice(0, 3)), (slice(7, 9), 0)):
         x_hi[rows, columns] = jnp.zeros_like(x_hi[rows, columns])
     for rows, columns in (
@@ -185,10 +190,10 @@
     cell = iota((1, 192), 1)
     patch = cell >> 5
     patch_column = (patch >= 3).astype(jnp.int32)
-    cell_row = (patch - 3 * patch_column) * 4 - 4 + ((cell >> 3) & 3)
+    cell_row = (patch - 3 * patch_column) * 4 - 4 + (cell & 3)
     for i, (first_patch, first_point) in enumerate(((0, 1), (-8, -3))):
         down = cell_row - ((point & 15) - 3)
-        right = (patch_column * 8 + first_patch + (cell & 7)) - ((point >> 4) + first_point)
+        right = (patch_column * 8 + first_patch + ((cell >> 2) & 7)) - ((point >> 4) + first_point)
         same = (down == 0) & (right == 0)
         near = (jnp.abs(down) <= 1) & (jnp.abs(right) <= 1) & (down + right != 0) | (
             (down == right) & (jnp.abs(down) == 1)
@@ -326,13 +331,22 @@
     for side in ACROSS:
         feature_copies[side].wait_recv()
     build(left=False)
+
+    @pl.when(jnp.logical_not(first))
+    def _():
+        pl.when(jnp.logical_not(last))(late)
+        build(left=True)
+
     for side in BACKWARD + ACROSS:
         vector_copies[side].wait_recv()
     first_step((1, 2))
     second_step((2,))
 
-    pl.when(jnp.logical_not(last))(late)
-    build(left=True)
+    @pl.when(first)
+    def _():
+        late()
+        build(left=True)
+
     for side in FORWARD:
         vector_copies[side].wait_recv()
     first_step((0,))

time: 28.2 us -> 27.3 us (0.968)
  Pallas kernels: 27.2 us -> 26.4 us
    pallas_call x1, Pallas kernels: 27.2 us -> 26.4 us  [per_device(): pl.pallas_call(kernel, name='filter', out_shape=jax.ShapeDtypeStruct((row...]
where the time goes in v5:
time: 27.3 us; the launch traced here: 27.1 us
  Pallas kernels  26.4 us (97%)
  local copies, waits for them, and re-layouts  0.76 us (3%)
    pallas_call x1, Pallas kernels, per_device(): pl.pallas_call(kernel, name='filter', out_shape=jax.ShapeDtypeStruct((row...  26.4 us
    unnamed x1, local copies, waits for them, and re-layouts  0.76 us

profile of v5, /device:TPU:39, one launch (start us, length us, event | category | flops | bytes accessed | tf_op | source)
XLA Modules:
  0.0 27.1 jit_solution(11404210450011048726)
XLA Ops:
  0.0 26.4 %filter.1 = f32[832,128]{1,0:T(8,128)S(1)} custom-call(bf16[4,8,128]{2,1,0:T(8,128)(2,1)} %features_hbm.1, s32[3,4,8]{2,1,0:T(4,128)} %bitcast.15, bf16[128,128]{1,0:T(8,128)(2,1)} %update_hbm.1, bf16[128,128]{1,0:T(8,128)(2,1)} %atom_hbm.1, bf16[128,128]{1,0:T(8,128)(2,1)} %pair_hbm.1, f32[4,128]{1,0:T(4,128)} %bias_hbm.1, bf16[169,128]{1,0:T(8,128)(2,1)} %bitcast.14, ...), custom_call_target="tpu_custom_call" | custom-call | tf_op jit(solution)/shard_map/filter/pallas_call | solution.py:369
  26.4 0.8 %copy.10 = f32[4,8,13,256]{3,1,2,0:T(8,128)} copy(f32[4,8,13,256]{3,1,2,0:T(8,128)S(1)} %bitcast.12) | data formatting | bytes 851968

commit v6 on v5

--- a/solution.py
+++ b/solution.py
@@ -288,20 +288,20 @@
 
         lax.fori_loop(0, 8, row, 0, unroll=UNROLL)
 
-    def second_step(groups):
+    def second_step(parts):
         def row(r, carry):
-            for g in groups:
-                c = 1 + 4 * g
-                value = (apply(y_hi, r, g) - CENTRE * y[r + 1, c : c + 4]) * (2.0 / HALF_WIDTH)
-                value = value - start(r + 1, c, 4)
-                z[r + 1, c : c + 4] = value
-                z_hi[r + 1, c : c + 4] = value.astype(BF16)
+            for g, begin, end in parts:
+                c, n = 1 + 4 * g + begin, end - begin
+                value = (apply(y_hi, r, g, begin, end) - CENTRE * y[r + 1, c : c + n]) * (2.0 / HALF_WIDTH)
+                value = value - start(r + 1, c, n)
+                z[r + 1, c : c + n] = value
+                z_hi[r + 1, c : c + n] = value.astype(BF16)
             return carry
 
         lax.fori_loop(1, 7, row, 0, unroll=UNROLL)
 
-    def third_row(r, carry):
-        for g, begin, end in ((0, 2, 4), (1, 0, 4), (2, 0, 2)):
+    def third_row(parts, r, carry):
+        for g, begin, end in parts:
             c, n = 1 + 4 * g + begin, end - begin
             value = (apply(z_hi, r, g, begin, end) - CENTRE * z[r + 1, c : c + n]) * (2.0 / HALF_WIDTH)
             value = value - y[r + 1, c : c + n]
@@ -312,6 +312,9 @@
                     ]
         return carry
 
+    def third_step(parts):
+        lax.fori_loop(2, 6, functools.partial(third_row, parts), 0, unroll=UNROLL)
+
     def late():
         def send_back():
             pl.semaphore_wait(answered, len(BACKWARD))
@@ -340,7 +343,8 @@
     for side in BACKWARD + ACROSS:
         vector_copies[side].wait_recv()
     first_step((1, 2))
-    second_step((2,))
+    second_step(((1, 1, 4), (2, 0, 3)))
+    third_step(((1, 2, 4), (2, 0, 2)))
 
     @pl.when(first)
     def _():
@@ -350,8 +354,8 @@
     for side in FORWARD:
         vector_copies[side].wait_recv()
     first_step((0,))
-    second_step((0, 1))
-    lax.fori_loop(2, 6, third_row, 0, unroll=UNROLL)
+    second_step(((0, 1, 4), (1, 0, 1)))
+    third_step(((0, 2, 4), (1, 0, 2)))
 
     for side in SIDES:
         feature_copies[side].wait_send()

time: 27.3 us -> 27.5 us (level)
  no operation moved by 1% of the time
where the time goes in v6:
time: 27.5 us; the launch traced here: 27.4 us
  Pallas kernels  26.6 us (97%)
  local copies, waits for them, and re-layouts  0.76 us (3%)
    pallas_call x1, Pallas kernels, per_device(): pl.pallas_call(kernel, name='filter', out_shape=jax.ShapeDtypeStruct((row...  26.6 us
    unnamed x1, local copies, waits for them, and re-layouts  0.76 us

profile of v6, /device:TPU:39, one launch (start us, length us, event | category | flops | bytes accessed | tf_op | source)
XLA Modules:
  0.0 27.4 jit_solution(10485189801102802105)
XLA Ops:
  0.0 26.6 %filter.1 = f32[832,128]{1,0:T(8,128)S(1)} custom-call(bf16[4,8,128]{2,1,0:T(8,128)(2,1)} %features_hbm.1, s32[3,4,8]{2,1,0:T(4,128)} %bitcast.15, bf16[128,128]{1,0:T(8,128)(2,1)} %update_hbm.1, bf16[128,128]{1,0:T(8,128)(2,1)} %atom_hbm.1, bf16[128,128]{1,0:T(8,128)(2,1)} %pair_hbm.1, f32[4,128]{1,0:T(4,128)} %bias_hbm.1, bf16[169,128]{1,0:T(8,128)(2,1)} %bitcast.14, ...), custom_call_target="tpu_custom_call" | custom-call | tf_op jit(solution)/shard_map/filter/pallas_call | solution.py:373
  26.6 0.8 %copy.10 = f32[4,8,13,256]{3,1,2,0:T(8,128)} copy(f32[4,8,13,256]{3,1,2,0:T(8,128)S(1)} %bitcast.12) | data formatting | bytes 851968
